TPU v7x, 32 devices: a whole 2x2x4 slice. The times are simulated.
32 devices in a mesh: dp: 8 (over y, x, core), seq: 4 (over z).
Axes of the slice: x: 2, y: 2, z: 4, core: 2. Of those that a mesh axis runs over, the one named last changes fastest.
Arguments:
- features: bfloat16 [8, 512, 2560], P('dp', 'seq'), may hold values from -6 to 6
- head_inputs: bfloat16 [8, 512, 2560], P('dp', 'seq'), may hold values from -6 to 6
- out_grad: bfloat16 [8, 512, 2560], P('dp', 'seq'), may hold values from -6 to 6
- bc_weight: bfloat16 [2560, 128], P('dp'), may hold values from -0.125 to 0.125
- dt_weight: bfloat16 [2560, 40], P('dp'), may hold values from -0.125 to 0.125
- dt_bias: float32 [40], replicated, may hold values from -7 to -5.5
- decay_rate: float32 [40], replicated, may hold values from 0.3125 to 16
- skip_gain: float32 [40], replicated, may hold values from 0.5 to 1.5
Outputs:
- input_grad: bfloat16 [8, 512, 2560], P('dp', 'seq')
- head_grad: bfloat16 [8, 512, 2560], P('dp', 'seq')
- bc_weight_grad: float32 [2560, 128], P('dp')
- dt_weight_grad: float32 [2560, 40], P('dp')
All inputs are finite; a program needn't handle non-finite values.
Results may differ from a plain program's by a relative error of at most 0.0049.
Values may be sent and summed in bfloat16 or wider, within the bound.
A program may use at most 128 MiB of HBM per device.

v0:
```python
import math

import jax
import jax.numpy as jnp
from jax import lax
from jax.sharding import PartitionSpec as P

highest = lax.Precision.HIGHEST


def entering(value, axis, join, neutral, backward):
    count, mine = (lax.axis_size(axis), lax.axis_index(axis))
    pieces = jax.tree.map(lambda part: lax.all_gather(part, axis), value)
    if backward:
        pieces = jax.tree.map(lambda part: part[::-1], pieces)
        mine = count - 1 - mine
    total = jax.tree.map(
        lambda part, zero: jnp.full_like(part, 0) + jnp.asarray(zero, part.dtype), value, neutral
    )

    def hop(position, total):
        longer = join(total, jax.tree.map(lambda part: part[position], pieces))
        return jax.tree.map(lambda new, old: jnp.where(position < mine, new, old), longer, total)

    return lax.fori_loop(0, count - 1, hop, total)


def spread_heads(values, head_size):
    return jnp.repeat(values, head_size, axis=-1)


def chain_link(earlier, later):
    decay_one, state_one = earlier
    decay_two, state_two = later
    head_size = state_one.shape[1] // decay_one.shape[0]
    factor = spread_heads(jnp.exp(decay_two), head_size)
    return (decay_one + decay_two, state_one * factor[None, :] + state_two)


def body(features, head_inputs, out_grad, bc_weight, dt_weight, dt_bias, decay_rate, skip_gain):
    tokens = features[0]
    inputs_f = head_inputs[0].astype(jnp.float32)
    cotangent = out_grad[0].astype(jnp.float32)
    heads = dt_bias.shape[0]
    inner = inputs_f.shape[1]
    head_size = inner // heads
    state = bc_weight.shape[1] // 2
    length = tokens.shape[0]
    joined = jnp.concatenate([bc_weight, dt_weight], axis=1)
    columns = tokens
    projection = jnp.dot(
        columns,
        lax.all_gather(joined, "dp", axis=0, tiled=True),
        preferred_element_type=jnp.float32,
    )
    b_rows = projection[:, :state]
    c_rows = projection[:, state : 2 * state]
    pre_step = projection[:, 2 * state :] + dt_bias[None, :]
    step_size = jax.nn.softplus(pre_step)
    log_decay = -decay_rate[None, :] * step_size
    cumulative = jnp.cumsum(log_decay, axis=0)
    total_decay = cumulative[-1]
    scaled_in = inputs_f * spread_heads(step_size, head_size)
    to_end = jnp.exp(total_decay[None, :] - cumulative)
    end_weight = spread_heads(to_end, head_size)
    scaled_end = scaled_in * end_weight
    local_state = jnp.dot(b_rows.T, scaled_end, precision=highest)
    from_start = jnp.exp(cumulative)
    weighted_grad = cotangent * spread_heads(from_start, head_size)
    returned_part = jnp.dot(c_rows.T, weighted_grad, precision=highest)
    identity = (jnp.zeros_like(total_decay), jnp.zeros_like(local_state))
    carried = entering((total_decay, local_state), "seq", chain_link, identity, False)
    returned = entering((total_decay, returned_part), "seq", chain_link, identity, True)
    state_in = carried[1]
    state_grad = returned[1]
    positions = jnp.arange(length)
    causal = positions[:, None] >= positions[None, :]
    gap = cumulative.T[:, :, None] - cumulative.T[:, None, :]
    weights_mat = jnp.exp(jnp.where(causal[None], gap, -1e30))
    intersection = jnp.dot(c_rows, b_rows.T, precision=highest)
    mixing = intersection[None] * weights_mat
    grad_view = cotangent.reshape(length, heads, head_size)
    input_view = scaled_in.reshape(length, heads, head_size)
    mixing_grad = jnp.einsum("thp,uhp->htu", grad_view, input_view, precision=highest)
    intersection_grad = jnp.sum(mixing_grad * weights_mat, axis=0)
    product = mixing_grad * mixing
    cum_grad = (jnp.sum(product, axis=2) - jnp.sum(product, axis=1)).T
    c_grad = jnp.dot(intersection_grad, b_rows, precision=highest)
    b_grad = jnp.dot(intersection_grad.T, c_rows, precision=highest)
    scaled_grad = jnp.einsum("htu,thp->uhp", mixing, grad_view, precision=highest).reshape(
        length, inner
    )
    inter_out = jnp.dot(c_rows, state_in, precision=highest)
    c_grad = c_grad + jnp.dot(weighted_grad, state_in.T, precision=highest)
    cum_grad = cum_grad + from_start * jnp.sum(
        (cotangent * inter_out).reshape(length, heads, head_size), axis=2
    )
    reach = jnp.dot(b_rows, state_grad, precision=highest)
    scaled_grad = scaled_grad + end_weight * reach
    b_grad = b_grad + jnp.dot(scaled_end, state_grad.T, precision=highest)
    to_end_grad = jnp.sum((scaled_in * reach).reshape(length, heads, head_size), axis=2) * to_end
    cum_grad = cum_grad - to_end_grad
    end_grad = jnp.sum(to_end_grad, axis=0) + jnp.exp(total_decay) * jnp.sum(
        (state_grad * state_in).reshape(state, heads, head_size), axis=(0, 2)
    )
    cum_grad = cum_grad.at[length - 1].add(end_grad)
    decay_grad = jnp.cumsum(cum_grad[::-1], axis=0)[::-1]
    step_grad = -decay_rate[None, :] * decay_grad + jnp.sum(
        (inputs_f * scaled_grad).reshape(length, heads, head_size), axis=2
    )
    pre_grad = step_grad * jax.nn.sigmoid(pre_step)
    head_grad = (
        cotangent * spread_heads(skip_gain, head_size)[None, :]
        + spread_heads(step_size, head_size) * scaled_grad
    ).astype(jnp.bfloat16)
    proj_grad = jnp.concatenate([b_grad, c_grad, pre_grad], axis=1).astype(jnp.bfloat16)
    input_grad = lax.dot_general(
        proj_grad,
        lax.all_gather(joined, "dp", axis=0, tiled=True),
        (((1,), (1,)), ((), ())),
        preferred_element_type=jnp.float32,
    )
    input_grad = input_grad.astype(jnp.bfloat16)
    columns = tokens
    owned = lax.psum_scatter(
        lax.dot_general(
            columns, proj_grad, (((0,), (0,)), ((), ())), preferred_element_type=jnp.float32
        ),
        "dp",
        scatter_dimension=0,
        tiled=True,
    )
    summed = lax.psum(owned, "seq")
    summed = summed * (1.0 / math.sqrt(lax.axis_size("dp") * lax.axis_size("seq") * length))
    return (input_grad[None], head_grad[None], summed[:, : 2 * state], summed[:, 2 * state :])


def solution(mesh):
    in_specs = (
        P("dp", "seq", None),
        P("dp", "seq", None),
        P("dp", "seq", None),
        P("dp", None),
        P("dp", None),
        P(),
        P(),
        P(),
    )
    out_specs = (P("dp", "seq", None), P("dp", "seq", None), P("dp", None), P("dp", None))
    return jax.shard_map(body, mesh=mesh, in_specs=in_specs, out_specs=out_specs, check_vma=False)
```

profile of v0, /device:TPU:0, one launch (start us, length us, event | category | flops | bytes accessed | tf_op | source)
XLA Modules:
  0.0 269.6 jit_solution(1364915673814624190)
XLA Ops:
  9.7 12.4 %all-gather.2 = bf16[8,320,168]{1,2,0:T(8,128)(2,1)S(1)} all-gather(bf16[1,320,168]{1,2,0:T(8,128)(2,1)S(1)} %maximum_bitcast_fusion), channel_id=1, replica_groups=mesh['dp'=8,'seq'=4] {'dp'}, dimensions={0}, use_global_device_ids=true | all-gather | bytes 967680 | tf_op jit(solution)/shard_map/all_gather | solution.py:53
  25.0 1.8 copy.161
  28.9 11.1 %all-gather.3 = f32[4,1,40]{2,1,0:T(1,128)S(1)} all-gather(f32[1,1,40]{2,1,0:T(1,128)S(1)} %bitcast.115), channel_id=1, replica_groups=mesh['dp'=8,'seq'=4] {'seq'}, dimensions={0}, use_global_device_ids=true | all-gather | bytes 800 | tf_op jit(solution)/shard_map/all_gather | solution.py:13
  42.9 41.0 %all-gather.7.cloned.1.call-done = f32[256,2560]{1,0:T(8,128)} async-done(((f32[64,2560]{1,0:T(8,128)}), f32[256,2560]{1,0:T(8,128)}) %all-gather.7.cloned.1.call-update) | async-done | bytes 2621456 | tf_op jit(solution)/shard_map/all_gather | solution.py:13
  83.9 3.4 %rev.13 = f32[4,64,2560]{2,1,0:T(8,128)} reverse(f32[4,64,2560]{2,1,0:T(8,128)} %bitcast.107), dimensions={0} | reverse | bytes 5242880 | tf_op jit(solution)/shard_map/rev | solution.py:15
  87.4 5.5 %while.29 = (s32[]{:T(128)}, f32[64,2560]{1,0:T(8,128)S(1)}, s32[]{:T(128)}, f32[4,40]{1,0:T(4,128)S(1)}, f32[4,64,2560]{2,1,0:T(8,128)}, /*index=5*/s32[]{:T(128)}, s32[]{:T(128)}) while((s32[]{:T(128)}, f32[64,2560]{1,0:T(8,128)S(1)}, s32[]{:T(128)}, f32[4,40]{1,0:T(4,128)S(1)}, f32[4,64,2560]{2,1,0:T(8,128)}, ...), condition=%wide.region_3.4_spmd.clone, body=%wide.region_2.3_spmd.clone.sunk | while | flops 655364 | bytes 2007633 | solution.py:25
  92.8 3.9 %fusion.26 = (f32[128,2560]{1,0:T(8,128)}, f32[128,2560]{1,0:T(8,128)}) fusion(f32[128,2560]{1,0:T(8,128)S(1)} %copy.156, bf16[1,128,2560]{2,1,0:T(8,128)(2,1)} %param.15, f32[64,2560]{1,0:T(8,128)S(1)} %get-tuple-element.204, f32[128,168]{0,1:T(8,128)S(1)} %convolution_bitcast_fusion.1), kind=kOutput, calls=%fused_computation.43 | convolution fusion | flops 252641280 | bytes 5275648 | tf_op jit(solution)/shard_map/dot_general | solution.py:98
  96.8 2.8 %copy.164 = f32[128,2560]{0,1:T(8,128)} copy(f32[128,2560]{1,0:T(8,128)} %get-tuple-element.299) | data formatting | bytes 2621440 | tf_op jit(solution)/shard_map/mul | solution.py:101
  102.8 2.8 %copy.159 = f32[128,2560]{1,0:T(8,128)} copy(f32[128,2560]{0,1:T(8,128)} %bitcast.105) | data formatting | bytes 2621440 | tf_op jit(solution)/shard_map/reshape | solution.py:29
  105.6 3.3 %fusion.29 = f32[64,2560]{1,0:T(8,128)} fusion(f32[128,2560]{1,0:T(8,128)} %copy.159, f32[128,2560]{1,0:T(8,128)S(1)} %copy.156, bf16[1,128,2560]{2,1,0:T(8,128)(2,1)} %param.15, f32[128,168]{0,1:T(8,128)S(1)} %convolution_bitcast_fusion.1), kind=kOutput, calls=%fused_computation.47 | convolution fusion | flops 252641280 | bytes 3964928 | tf_op jit(solution)/shard_map/dot_general | solution.py:67
  110.2 2.4 copy.149
  113.2 5.2 %fusion.5 = f32[40,128,64]{1,2,0:T(8,128)} fusion(bf16[128,40,64]{0,2,1:T(8,128)(2,1)} %bitcast.110, f32[128,128]{0,1:T(8,128)S(1)} %fusion.34, f32[40,128]{1,0:T(8,128)S(1)} %copy.154, pred[128,128]{0,1:T(8,128)(4,1)S(1)} %iota_compare_fusion), kind=kOutput, calls=%fused_computation.15 | convolution fusion | flops 505282560 | bytes 2068480 | tf_op jit(solution)/shard_map/htu,thp->uhp/dot_general | solution.py:90
  118.4 2.9 %copy.171 = f32[128,2560]{1,0:T(8,128)} copy(f32[128,2560]{0,1:T(8,128)} %bitcast.108) | data formatting | bytes 2621440 | tf_op jit(solution)/shard_map/reshape | solution.py:90
  121.3 5.8 %fusion.7 = (f32[40,128]{1,0:T(8,128)}, f32[40,128]{1,0:T(8,128)}, f32[128,128]{0,1:T(8,128)S(1)}) fusion(f32[128,128]{0,1:T(8,128)S(1)} %fusion.34, f32[40,128]{1,0:T(8,128)S(1)} %copy.154, pred[128,128]{0,1:T(8,128)(4,1)} %copy-done.11, bf16[128,40,64]{0,2,1:T(8,128)(2,1)} %bitcast.111, f32[128,40,64]{0,2,1:T(8,128)} %bitcast.109, ...), kind=kOutput, calls=%fused_computation.18 | convolution fusion | flops 508860416 | bytes 2195456 | tf_op jit(solution)/shard_map/thp,uhp->htu/dot_general | solution.py:84
  128.9 4.4 %fusion.21 = (bf16[1,128,2560]{2,1,0:T(8,128)(2,1)}, f32[128,2560]{1,0:T(8,128)}) fusion(f32[128,2560]{1,0:T(8,128)S(1)} %copy.156, bf16[1,128,2560]{2,1,0:T(8,128)(2,1)} %param.16, f32[2560]{0:T(1024)S(1)} %mul.155, f32[128,2560]{1,0:T(8,128)} %copy.171, f32[128,2560]{1,0:T(8,128)} %copy.159, f32[128,2560]{1,0:T(8,128)} %get-tuple-element.300, ...), kind=kLoop, calls=%fused_computation.38 | loop fusion | flops 2949120 | bytes 8529920 | tf_op jit(solution)/shard_map/broadcast_in_dim | solution.py:135
  133.2 2.8 %copy.172 = f32[128,2560]{0,1:T(8,128)} copy(f32[128,2560]{1,0:T(8,128)} %get-tuple-element.298) | data formatting | bytes 2621440 | tf_op jit(solution)/shard_map/mul | solution.py:109
  136.0 2.0 reduce_sum.94
  138.1 3.0 %fusion.18 = bf16[128,64]{0,1:T(8,128)(2,1)S(1)} fusion(f32[128,64]{0,1:T(8,128)S(1)} %fusion.42, f32[64,2560]{1,0:T(8,128)S(1)} %get-tuple-element.204, f32[128,2560]{1,0:T(8,128)} %copy.159, f32[128,2560]{1,0:T(8,128)S(1)} %copy.156, bf16[1,128,2560]{2,1,0:T(8,128)(2,1)} %param.15), kind=kOutput, calls=%fused_computation.35 | convolution fusion | flops 252657664 | bytes 3981312 | tf_op jit(solution)/shard_map/dot_general | solution.py:100
  141.1 21.6 %all-gather.9.cloned.1.call-done = f32[256,2560]{1,0:T(8,128)} async-done(((f32[64,2560]{1,0:T(8,128)}), f32[256,2560]{1,0:T(8,128)}) %all-gather.9.cloned.1.call-update) | async-done | bytes 2621456 | tf_op jit(solution)/shard_map/all_gather | solution.py:13
  162.7 7.3 %while.30 = (s32[]{:T(128)}, f32[64,2560]{1,0:T(8,128)S(1)}, s32[]{:T(128)}, f32[4,40]{1,0:T(4,128)}, f32[4,64,2560]{2,1,0:T(8,128)}, /*index=5*/s32[]{:T(128)}, s32[]{:T(128)}) while((s32[]{:T(128)}, f32[64,2560]{1,0:T(8,128)S(1)}, s32[]{:T(128)}, f32[4,40]{1,0:T(4,128)}, f32[4,64,2560]{2,1,0:T(8,128)}, /*index=5*/s32[]{:T(128)}, ...), condition=%wide.region_5.6_spmd.clone, body=%wide.region_4.5_spmd.clone.sunk | while | flops 655364 | bytes 2007633 | solution.py:25
  178.6 2.0 copy.177
  180.7 42.5 %reduce-scatter.4.cloned.1.call-done = f32[320,168]{1,0:T(8,128)} async-done(((f32[2560,168]{1,0:T(8,128)}), f32[320,168]{1,0:T(8,128)}) %reduce-scatter.4.cloned.1.call-update) | async-done | bytes 215056
  223.2 1.8 copy.178
  226.3 34.4 %all-reduce.2.cloned.1.call-done = f32[320,168]{0,1:T(8,128)} async-done(((f32[320,168]{0,1:T(8,128)}), f32[320,168]{0,1:T(8,128)}) %all-reduce.2.cloned.1.call-update) | async-done | bytes 215056 | tf_op jit(solution)/shard_map/psum | solution.py:133
  (122 shorter events, 41.9 us)
Async XLA Ops:
  7.2 15.8 %copy-start = (bf16[1,128,2560]{2,1,0:T(8,128)(2,1)S(1)}, bf16[1,128,2560]{2,1,0:T(8,128)(2,1)}, u32[]{:S(2)}) copy-start(bf16[1,128,2560]{2,1,0:T(8,128)(2,1)} %param.14) | copy-start | bytes 1966084
  7.2 76.7 %all-gather.7.cloned.1.call-start = ((), (), s32[]{:S(2)}) async-start(), calls=%async_computation.2 | async-start | bytes 3276800 | tf_op jit(solution)/shard_map/all_gather | solution.py:13
  7.9 15.4 %copy-start.15 = (f32[40]{0:T(128)}, f32[40]{0:T(128)S(1)}, u32[]{:S(2)}) copy-start(f32[40]{0:T(128)S(1)} %neg.13) | copy-start | bytes 484
  22.3 1.1 copy-start.13
  23.0 2.0 copy-start.5
  25.0 1.8 copy-start.1
  26.8 1.8 copy-start.3
  28.6 134.1 %all-gather.9.cloned.1.call-start = ((), (), s32[]{:S(2)}) async-start(), calls=%async_computation.3 | async-start | bytes 3276800 | tf_op jit(solution)/shard_map/all_gather | solution.py:13
  40.0 2.9 %copy-start.12 = (f32[4,1,40]{2,1,0:T(1,128)}, f32[4,1,40]{2,1,0:T(1,128)S(1)}, u32[]{:S(2)}) copy-start(f32[4,1,40]{2,1,0:T(1,128)S(1)} %all-gather.3) | copy-start | bytes 1924
  108.9 114.3 %reduce-scatter.4.cloned.1.call-start = ((), (), s32[]{:S(2)}) async-start(), calls=%async_computation.4 | async-start | bytes 2949120
  110.2 2.4 copy-start.17
  112.9 5.5 %copy-start.11 = (pred[128,128]{0,1:T(8,128)(4,1)}, pred[128,128]{0,1:T(8,128)(4,1)S(1)}, u32[]{:S(2)}) copy-start(pred[128,128]{0,1:T(8,128)(4,1)S(1)} %iota_compare_fusion) | copy-start | bytes 49156
  170.1 1.1 copy-start.2
  171.1 1.3 copy-start.4
  175.7 1.5 copy-start.9
  175.7 1.5 copy-start.10
  175.7 1.6 copy-start.7
  175.7 2.4 copy-start.8
  175.7 2.4 copy-start.14
  175.7 2.4 copy-start.16
  180.6 44.4 %copy-start.6 = (bf16[2560,168]{0,1:T(8,128)(2,1)S(1)}, bf16[2560,168]{0,1:T(8,128)(2,1)}, u32[]{:S(2)}) copy-start(bf16[2560,168]{0,1:T(8,128)(2,1)} %copy-done.5) | copy-start | bytes 2580484
  180.6 80.0 %all-reduce.2.cloned.1.call-start = ((), (), s32[]{:S(2)}) async-start(), calls=%async_computation.1 | async-start | bytes 516096 | tf_op jit(solution)/shard_map/psum | solution.py:133
Sparse Core Ops, SparseCore 0:
  28.7 55.1 all-gather.6
  109.1 53.5 all-gather.8
  180.8 42.4 reduce-scatter.3
  225.4 35.2 all-reduce.1
where the time goes:
time: 271 us; the launch traced here: 270 us
  waiting for transfers between devices  140 us (52%)
  local copies, waits for them, and re-layouts  40.3 us (15%)
  matrix products  28.4 us (10%)
  blocking collectives  23.5 us (9%)
  other arithmetic  23.2 us (9%)
  between operations  14.1 us (5%)
    all_gather x2, waiting for transfers between devices, entering(): pieces = jax.tree.map(lambda part: lax.all_gather(part, axis), value)  62.6 us
    unnamed x5, waiting for transfers between devices  42.6 us
    psum x1, waiting for transfers between devices, body(): summed = lax.psum(owned, 'seq')  34.4 us
    all_gather x1, blocking collectives, body(): lax.all_gather(joined, 'dp', axis=0, tiled=True)  12.4 us
    all_gather x1, blocking collectives, entering(): pieces = jax.tree.map(lambda part: lax.all_gather(part, axis), value)  11.1 us
    select_n x6, other arithmetic, hop(): jnp.where(position < mine, new, old)  9.88 us
    unnamed x42, local copies, waits for them, and re-layouts  8.55 us
    reshape x3, local copies, waits for them, and re-layouts, spread_heads(): return jnp.repeat(values, head_size, axis=-1)  6.3 us
  transfers between devices with their start and end apart: 4, of which 4 were waited for; matrix products, arithmetic and copies ran while one was open for 13% of the time, Pallas kernels for 0%

commit v1 on v0

v1 whole, which is shorter than its diff:
```python
import functools
import math

import jax
import jax.numpy as jnp
from jax import lax
from jax.experimental import pallas as pl
from jax.experimental.pallas import tpu as pltpu
from jax.sharding import PartitionSpec as P

MESH = pl.DeviceIdType.MESH
F32, BF16 = jnp.float32, jnp.bfloat16
LANES = 128
CHUNK = 512
HIGHEST = lax.Precision.HIGHEST
NT = (((1,), (1,)), ((), ()))
TN = (((0,), (0,)), ((), ()))


def halves(value):
    high = value.astype(BF16)
    return high, (value - high.astype(F32)).astype(BF16)


def mm(left, right, dims=None):
    if dims is None:
        return jnp.dot(left, right, preferred_element_type=F32)
    return lax.dot_general(left, right, dims, preferred_element_type=F32)


def iota(shape, dim):
    return lax.broadcasted_iota(jnp.int32, shape, dim)


def kernel(
    dp, seq, heads, scale,
    f_ref, x_ref, g_ref, wbc_ref, wdt_ref, bias_ref, decay_ref, skip_ref,
    ig_ref, hg_ref, bcg_ref, dtg_ref, *,
    wall, par, pre_s, step_s, cum_s, cumt_s, ecum_s, toend_s, proj_s, bct_s, inter_s, rows_s,
    ig_acc, step_w, ecum_w, toend_w, end_w, wgrad, sgrad, left_s, right_s,
    fin, bin_, fout, bout, red_s, bg_s, cg_s, gp_s,
    gw, gw_out, rb1, s_out, rb2, zout, zin, final,
    ag_send, ag_recv, fw_send, fw_recv, ch_send, ch_recv,
    r1_send, r1_recv, r2_send, r2_recv, zr_send, zr_recv, za_send, za_recv,
):
    me, z = lax.axis_index("dp"), lax.axis_index("seq")
    last = seq - 1
    half = dp // 2
    sib = me + 1 - 2 * lax.rem(me, 2)
    length, inner = x_ref.shape
    rows = wbc_ref.shape[0]
    state = wbc_ref.shape[1] // 2
    head_size = inner // heads
    chunks = inner // CHUNK
    piece = -(-rows // (16 * seq)) * 16
    owners = -(-rows // piece)

    def at_dp(target):
        return (target, z)

    def peer(k):
        return lax.rem(me + 2 * k, dp)

    def source(k):
        return lax.rem(me + dp - 2 * k, dp)

    barrier = pltpu.get_barrier_semaphore()
    pl.semaphore_signal(barrier, inc=1, device_id=at_dp(sib), device_id_type=MESH)
    for k in range(1, half):
        pl.semaphore_signal(barrier, inc=1, device_id=at_dp(peer(k)), device_id_type=MESH)
    for k in range(1, seq):
        pl.semaphore_signal(barrier, inc=1, device_id=(me, lax.rem(z + k, seq)), device_id_type=MESH)

    def block(index):
        return pl.ds(pl.multiple_of(index * rows, 16), rows)

    wall[block(me), 0:LANES] = wbc_ref[...]
    wide = jnp.concatenate(
        [wdt_ref[...].astype(F32), jnp.zeros((rows, LANES - heads), F32)], axis=1
    )
    wall[block(me), LANES:] = wide.astype(BF16)
    par[...] = jnp.zeros_like(par)
    par[0:1, 0:heads] = bias_ref[...]
    par[1:2, 0:heads] = decay_ref[...]
    par[2:3, 0:heads] = skip_ref[...]
    pl.semaphore_wait(barrier, half + seq - 1)

    def ag_copy(k, owner, target):
        return pltpu.make_async_remote_copy(
            src_ref=wall.at[block(owner)], dst_ref=wall.at[block(owner)],
            send_sem=ag_send.at[k], recv_sem=ag_recv.at[k],
            device_id=at_dp(target), device_id_type=MESH,
        )

    def fw_copy(k, owner):
        return pltpu.make_async_remote_copy(
            src_ref=wall.at[block(owner)], dst_ref=wall.at[block(owner)],
            send_sem=fw_send.at[k], recv_sem=fw_recv.at[k],
            device_id=at_dp(sib), device_id_type=MESH,
        )

    for k in range(1, half):
        ag_copy(k, me, peer(k)).start()
    ag_copy(0, me, sib).start()
    for k in range(1, half):
        ag_copy(k, source(k), peer(k)).wait_recv()
        fw_copy(k, source(k)).start()
    ag_copy(0, sib, sib).wait_recv()
    for k in range(1, half):
        fw_copy(k, lax.rem(sib + dp - 2 * k, dp)).wait_recv()

    projection = mm(f_ref[...], wall[...])
    proj_s[...] = projection[:, :LANES]
    pre = projection[:, LANES:] + par[0:1, :]
    pre_s[...] = pre
    step = jnp.maximum(pre, 0.0) + jnp.log1p(jnp.exp(-jnp.abs(pre)))
    step_s[...] = step
    lower = (iota((length, length), 0) >= iota((length, length), 1)).astype(F32)
    cum = jnp.dot(
        lower, -par[1:2, :] * step, precision=HIGHEST, preferred_element_type=F32
    )
    cum_s[...] = cum
    cumt_s[...] = cum.T
    ecum_s[...] = jnp.exp(cum)
    toend_s[...] = jnp.exp(cum[length - 1 :, :] - cum)
    bct_s[...] = proj_s[...].T
    bt = bct_s[0:state, :]
    ct = bct_s[state:, :]
    bt_hi, bt_lo = halves(bt)
    ct_hi, ct_lo = halves(ct)
    bt3 = jnp.concatenate([bt_hi, bt_lo, bt_hi], axis=1)
    ct3 = jnp.concatenate([ct_hi, ct_lo, ct_hi], axis=1)
    b_rows = proj_s[:, 0:state]
    c_rows = proj_s[:, state:]
    inter_s[...] = jnp.dot(b_rows, ct, precision=HIGHEST, preferred_element_type=F32)

    def spread(value, c):
        high, low = halves(value)
        row = iota((LANES, CHUNK), 0)
        hot = (row == c * (CHUNK // head_size) + iota((LANES, CHUNK), 1) // head_size)
        hot = hot.astype(F32).astype(BF16)
        return mm(jnp.concatenate([high, low], axis=1), jnp.concatenate([hot, hot], axis=0))

    def lanes(c):
        return pl.ds(pl.multiple_of(c * CHUNK, CHUNK), CHUNK)

    @pl.loop(0, chunks)
    def _(c):
        cs = lanes(c)
        step_c = spread(step_s[...], c)
        ecum_c = spread(ecum_s[...], c)
        toend_c = spread(toend_s[...], c)
        ends = x_ref[:, cs].astype(F32) * step_c * toend_c
        weighted = g_ref[:, cs].astype(F32) * ecum_c
        step_w[:, cs] = step_c
        ecum_w[:, cs] = ecum_c
        toend_w[:, cs] = toend_c
        end_w[:, cs] = ends
        wgrad[:, cs] = weighted
        e_hi, e_lo = halves(ends)
        w_hi, w_lo = halves(weighted)
        left_s[c] = mm(bt3, jnp.concatenate([e_hi, e_hi, e_lo], axis=0))
        right_s[c] = mm(ct3, jnp.concatenate([w_hi, w_hi, w_lo], axis=0))

    def chain_copy(way, c):
        src, dst = ((fout, fin), (bout, bin_))[way]
        to = (z + 1, z + last)[way]
        return pltpu.make_async_remote_copy(
            src_ref=src.at[c], dst_ref=dst.at[c],
            send_sem=ch_send.at[way, c], recv_sem=ch_recv.at[way, c],
            device_id=(me, lax.rem(to, seq)), device_id_type=MESH,
        )

    def chain_hop(way, c):
        arrived, leaving, local = ((fin, fout, left_s), (bin_, bout, right_s))[way]
        first, final_one = ((0, last), (last, 0))[way]

        @pl.when(z == first)
        def _():
            arrived[c] = jnp.zeros((state, CHUNK), arrived.dtype)
            if seq > 1:
                leaving[c] = local[c].astype(leaving.dtype)
                chain_copy(way, c).start()

        @pl.when(z != first)
        def _():
            chain_copy(way, c).wait_recv()

            @pl.when(z != final_one)
            def _():
                decay = ecum_w[length - 1 :, lanes(c)]
                leaving[c] = (arrived[c].astype(F32) * decay + local[c]).astype(leaving.dtype)
                chain_copy(way, c).start()

    later = iota((length, length), 1) >= iota((length, length), 0)
    low_half = iota((length, LANES), 1) < head_size
    per_tile = LANES // head_size

    def tile_work(tile):
        ts = pl.ds(pl.multiple_of(tile * LANES, LANES), LANES)
        x_tile, g_tile = x_ref[:, ts].astype(F32), g_ref[:, ts].astype(F32)
        g_full = g_ref[:, ts]
        step, cum, inter = step_s[...], cum_s[...], inter_s[...]
        mixes, grads = [], []
        for part in range(per_tile):
            head = tile * per_tile + part
            pick = iota((length, LANES), 1) == head
            cum_col = jnp.sum(jnp.where(pick, cum, 0.0), axis=1, keepdims=True)
            step_col = jnp.sum(jnp.where(pick, step, 0.0), axis=1, keepdims=True)
            gap = cumt_s[pl.ds(head, 1), :] - cum_col
            weights = jnp.exp(jnp.where(later, gap, -1e30))
            mine = low_half if part == 0 else jnp.logical_not(low_half)
            x_part = jnp.where(mine, x_tile, 0.0).astype(BF16)
            g_part = jnp.where(mine, g_tile, 0.0).astype(BF16)
            mixing_grad = mm(x_part, g_full, NT) * step_col
            shared = mixing_grad * weights
            ig_acc[...] += shared
            rows_s[pl.ds(head, 1), :] = jnp.sum(shared * inter, axis=0, keepdims=True)
            mixes += list(halves(inter * weights))
            grads += [g_part, g_part]
        sgrad[:, ts] = mm(jnp.concatenate(mixes, axis=1), jnp.concatenate(grads, axis=0))

    def reduce_heads(value, c):
        lane = iota((LANES, CHUNK), 0)
        hot = lane == c * (CHUNK // head_size) + iota((LANES, CHUNK), 1) // head_size
        hot = hot.astype(F32).astype(BF16)
        high, low = halves(value)
        return mm(jnp.concatenate([high, low], axis=1), jnp.concatenate([hot, hot], axis=1), NT)

    b_hi, b_lo = halves(b_rows)
    c_hi, c_lo = halves(c_rows)
    bpair = jnp.concatenate([b_hi, b_lo], axis=1)
    cpair = jnp.concatenate([c_hi, c_lo], axis=1)

    def carried_work(c):
        cs = lanes(c)
        state_in, state_grad = fin[c], bin_[c]
        weighted, ends = wgrad[:, cs], end_w[:, cs]
        inter_out = mm(cpair, jnp.concatenate([state_in, state_in], axis=0))
        reach = mm(bpair, jnp.concatenate([state_grad, state_grad], axis=0))
        w_hi, w_lo = halves(weighted)
        e_hi, e_lo = halves(ends)
        cg_s[...] += mm(w_hi, state_in, NT) + mm(w_lo, state_in, NT)
        bg_s[...] += mm(e_hi, state_grad, NT) + mm(e_lo, state_grad, NT)
        total = sgrad[:, cs] + toend_w[:, cs] * reach
        x_part, g_part = x_ref[:, cs].astype(F32), g_ref[:, cs].astype(F32)
        decay = ecum_w[length - 1 :, cs]
        product = state_grad.astype(F32) * state_in.astype(F32)
        at_end = jnp.sum(ends * reach, axis=0, keepdims=True) + decay * jnp.sum(
            product, axis=0, keepdims=True
        )
        stacked = jnp.concatenate(
            [weighted * inter_out, x_part * total, jnp.broadcast_to(at_end, (8, CHUNK))], axis=0
        )
        red_s[...] += reduce_heads(stacked, c)
        skip_c = spread(jnp.broadcast_to(par[2:3, :], (8, LANES)), c)[0:1, :]
        hg_ref[:, cs] = (g_part * skip_c + step_w[:, cs] * total).astype(BF16)

    ig_acc[...] = jnp.zeros_like(ig_acc)
    rows_s[...] = jnp.zeros_like(rows_s)
    cg_s[...] = jnp.zeros_like(cg_s)
    bg_s[...] = jnp.zeros_like(bg_s)
    red_s[...] = jnp.zeros_like(red_s)
    tiles = CHUNK // LANES

    @pl.loop(0, chunks + last)
    def _(s):
        forward, back = s - z, s - (last - z)

        @pl.when(jnp.logical_and(forward >= 0, forward < chunks))
        def _():
            chain_hop(0, forward)

        @pl.when(jnp.logical_and(back >= 0, back < chunks))
        def _():
            chain_hop(1, back)

        @pl.when(s < chunks)
        def _():
            for tile in range(tiles):
                tile_work(s * tiles + tile)

        both = s - jnp.maximum(z, last - z)

        @pl.when(jnp.logical_and(both >= 0, both < chunks))
        def _():
            carried_work(both)

    acc = ig_acc[...]
    c_grad = cg_s[...] + lax.dot_general(
        acc, b_rows, TN, precision=HIGHEST, preferred_element_type=F32
    )
    b_grad = bg_s[...] + jnp.dot(acc, c_rows, precision=HIGHEST, preferred_element_type=F32)
    step = step_s[...]
    direct = red_s[length : 2 * length, :]
    cum_grad = rows_s[...].T + red_s[0:length, :] - step * direct
    is_last = iota((length, LANES), 0) == length - 1
    cum_grad = cum_grad + jnp.where(is_last, red_s[2 * length : 2 * length + 1, :], 0.0)
    upper = later.astype(F32)
    decay_grad = jnp.dot(upper, cum_grad, precision=HIGHEST, preferred_element_type=F32)
    step_grad = direct - par[1:2, :] * decay_grad
    pre_grad = step_grad / (1.0 + jnp.exp(-pre_s[...]))
    gp_s[:, 0:LANES] = jnp.concatenate([b_grad, c_grad], axis=1).astype(BF16)
    gp_s[:, LANES:] = pre_grad.astype(BF16)
    gproj = gp_s[...]

    for c in range(chunks):
        part = mm(f_ref[:, c * CHUNK : (c + 1) * CHUNK], gproj, TN)
        gw[c * CHUNK : (c + 1) * CHUNK, :] = part
        gw_out[c * CHUNK : (c + 1) * CHUNK, :] = part.astype(BF16)

    def r1_copy(k, owner):
        return pltpu.make_async_remote_copy(
            src_ref=gw_out.at[block(owner)], dst_ref=rb1.at[k],
            send_sem=r1_send.at[k], recv_sem=r1_recv.at[k],
            device_id=at_dp(sib), device_id_type=MESH,
        )

    def r2_copy(k, target):
        return pltpu.make_async_remote_copy(
            src_ref=s_out.at[k], dst_ref=rb2.at[k],
            send_sem=r2_send.at[k], recv_sem=r2_recv.at[k],
            device_id=at_dp(target), device_id_type=MESH,
        )

    order = list(range(1, half)) + [0]
    for k in order:
        r1_copy(k, lax.rem(sib + 2 * k, dp)).start()
    for k in order[:-1]:
        r1_copy(k, sib).wait_recv()
        s_out[k] = (gw[block(peer(k)), :] + rb1[k].astype(F32)).astype(BF16)
        r2_copy(k, peer(k)).start()

    for c in range(chunks):
        cs = slice(c * CHUNK, (c + 1) * CHUNK)
        ig_ref[:, cs] = mm(gproj, wall[cs, :], NT).astype(BF16)

    r1_copy(0, sib).wait_recv()
    total = gw[block(me), :] + rb1[0].astype(F32)
    for k in range(1, half):
        r2_copy(k, peer(k)).wait_recv()
        total = total + rb2[k].astype(F32)

    zout[...] = total.astype(zout.dtype)

    def z_piece(index):
        return pl.ds(pl.multiple_of(index * piece, 16), piece)

    def to_z(k):
        return lax.rem(z + k, seq)

    def from_z(k):
        return lax.rem(z + seq - k, seq)

    def zr_copy(k):
        return pltpu.make_async_remote_copy(
            src_ref=zout.at[z_piece(to_z(k))], dst_ref=zin.at[k],
            send_sem=zr_send.at[k], recv_sem=zr_recv.at[k],
            device_id=(me, to_z(k)), device_id_type=MESH,
        )

    def za_copy(k, owner):
        return pltpu.make_async_remote_copy(
            src_ref=final.at[z_piece(owner)], dst_ref=final.at[z_piece(owner)],
            send_sem=za_send.at[k], recv_sem=za_recv.at[k],
            device_id=(me, to_z(k)), device_id_type=MESH,
        )

    owner_here = z < owners
    for k in range(1, seq):
        @pl.when(to_z(k) < owners)
        def _():
            zr_copy(k).start()

    @pl.when(owner_here)
    def _():
        mine = zout[z_piece(z), :].astype(F32)
        for k in range(1, seq):
            zr_copy(k).wait_recv()
            mine = mine + zin[k].astype(F32)
        final[z_piece(z), :] = mine * scale
        for k in range(1, seq):
            za_copy(k, z).start()

    for k in range(1, seq):
        @pl.when(from_z(k) < owners)
        def _():
            za_copy(k, from_z(k)).wait_recv()

    bcg_ref[...] = final[:, 0:LANES]
    dtg_ref[...] = final[:, LANES : LANES + heads]

    ag_copy(0, me, sib).wait_send()
    for k in range(1, half):
        ag_copy(k, me, peer(k)).wait_send()
        fw_copy(k, source(k)).wait_send()
        r2_copy(k, peer(k)).wait_send()
    for k in range(half):
        r1_copy(k, sib).wait_send()
    for k in range(1, seq):
        @pl.when(to_z(k) < owners)
        def _():
            zr_copy(k).wait_send()

    @pl.when(owner_here)
    def _():
        for k in range(1, seq):
            za_copy(k, z).wait_send()

    for way, final_one in ((0, last), (1, 0)):
        @pl.when(z != final_one)
        def _():
            @pl.loop(0, chunks)
            def _(c):
                chain_copy(way, c).wait_send()


def body(dp, seq, features, head_inputs, out_grad, bc_weight, dt_weight, dt_bias, decay_rate, skip_gain):
    _, length, width = features.shape
    inner = head_inputs.shape[2]
    heads = dt_bias.shape[0]
    rows, both = bc_weight.shape
    state = both // 2
    half = dp // 2
    chunks = inner // CHUNK
    piece = -(-rows // (16 * seq)) * 16
    scale = 1.0 / math.sqrt(dp * seq * length)
    vmem, dma = pltpu.VMEM, pltpu.SemaphoreType.DMA
    square = vmem((length, LANES), F32)
    broad = vmem((length, inner), F32)
    states = vmem((chunks, state, CHUNK), F32)
    wire = vmem((chunks, state, CHUNK), BF16)
    narrow = vmem((length, state), F32)
    scratch = dict(
        wall=vmem((width, 2 * LANES), BF16), par=vmem((8, LANES), F32),
        pre_s=square, step_s=square, cum_s=square, cumt_s=square, ecum_s=square,
        toend_s=square, proj_s=square, bct_s=square, inter_s=square, rows_s=square,
        ig_acc=square,
        step_w=broad, ecum_w=broad, toend_w=broad, end_w=broad, wgrad=broad, sgrad=broad,
        left_s=states, right_s=states,
        fin=wire, bin_=wire, fout=wire, bout=wire,
        red_s=vmem((2 * length + 8, LANES), F32), bg_s=narrow, cg_s=narrow,
        gp_s=vmem((length, 2 * LANES), BF16),
        gw=vmem((width, 2 * LANES), F32), gw_out=vmem((width, 2 * LANES), BF16),
        rb1=vmem((half, rows, 2 * LANES), BF16), s_out=vmem((half, rows, 2 * LANES), BF16),
        rb2=vmem((half, rows, 2 * LANES), BF16),
        zout=vmem((rows, 2 * LANES), BF16), zin=vmem((seq, piece, 2 * LANES), BF16),
        final=vmem((rows, 2 * LANES), F32),
        ag_send=dma((half,)), ag_recv=dma((half,)), fw_send=dma((half,)), fw_recv=dma((half,)),
        ch_send=dma((2, chunks)), ch_recv=dma((2, chunks)),
        r1_send=dma((half,)), r1_recv=dma((half,)), r2_send=dma((half,)), r2_recv=dma((half,)),
        zr_send=dma((seq,)), zr_recv=dma((seq,)), za_send=dma((seq,)), za_recv=dma((seq,)),
    )
    whole = pl.BlockSpec(memory_space=pltpu.VMEM)
    results = pl.pallas_call(
        functools.partial(kernel, dp, seq, heads, scale),
        out_shape=(
            jax.ShapeDtypeStruct((length, width), BF16),
            jax.ShapeDtypeStruct((length, inner), BF16),
            jax.ShapeDtypeStruct((rows, both), F32),
            jax.ShapeDtypeStruct((rows, heads), F32),
        ),
        in_specs=[whole] * 8,
        out_specs=(whole,) * 4,
        scratch_shapes=scratch,
        compiler_params=pltpu.CompilerParams(
            collective_id=0, has_side_effects=True, vmem_limit_bytes=48 * 2**20
        ),
        name="mixer_backward",
    )(
        features[0], head_inputs[0], out_grad[0], bc_weight, dt_weight,
        dt_bias[None, :], decay_rate[None, :], skip_gain[None, :],
    )
    input_grad, head_grad, bc_grad, dt_grad = results
    return input_grad[None], head_grad[None], bc_grad, dt_grad


def solution(mesh):
    tokens = P("dp", "seq", None)
    return jax.shard_map(
        functools.partial(body, mesh.shape["dp"], mesh.shape["seq"]),
        mesh=mesh,
        in_specs=(tokens, tokens, tokens, P("dp", None), P("dp", None), P(), P(), P()),
        out_specs=(tokens, tokens, P("dp", None), P("dp", None)),
        check_vma=False,
    )
```

time: 271 us -> 72.9 us (0.27)
  waiting for transfers between devices: 140 us -> 0 us
  Pallas kernels: 0 us -> 64.6 us
  local copies, waits for them, and re-layouts: 40.3 us -> 7.26 us
  matrix products: 28.4 us -> 0 us
  blocking collectives: 23.5 us -> 0 us
  other arithmetic: 23.2 us -> 0 us
  between operations: 14.1 us -> 0.72 us
    pallas_call x0 -> x1, Pallas kernels: none -> 64.6 us  [body(): pl.pallas_call(functools.partial(kernel, dp, seq, heads, scale), out_shap...]
    all_gather x2 -> x0, waiting for transfers between devices: 62.6 us -> none  [entering(): pieces = jax.tree.map(lambda part: lax.all_gather(part, axis), value)]
    unnamed x5 -> x0, waiting for transfers between devices: 42.6 us -> none
    psum x1 -> x0, waiting for transfers between devices: 34.4 us -> none  [body(): summed = lax.psum(owned, 'seq')]
    dot_general x14 -> x0, matrix products: 28.4 us -> none  [the longest x1 5.76 us: body(): jnp.einsum('thp,uhp->htu', grad_view, input_view, precision=highest)]
    all_gather x2 -> x0, blocking collectives: 23.5 us -> none  [the longest x1 12.4 us: body(): lax.all_gather(joined, 'dp', axis=0, tiled=True)]
    select_n x6 -> x0, other arithmetic: 9.88 us -> none  [hop(): jnp.where(position < mine, new, old)]
    reshape x4 -> x0, local copies, waits for them, and re-layouts: 9.18 us -> none  [the longest x3 6.3 us: spread_heads(): return jnp.repeat(values, head_size, axis=-1)]
  transfers between devices with their start and end apart: 4 -> 0, of which waited for: 4 -> 0; matrix products, arithmetic and copies ran while one was open for 13% -> 0% of each run, Pallas kernels for 0% -> 0%
where the time goes in v1:
time: 72.9 us; the launch traced here: 72.6 us
  Pallas kernels  64.6 us (89%)
  local copies, waits for them, and re-layouts  7.26 us (10%)
    pallas_call x1, Pallas kernels, body(): pl.pallas_call(functools.partial(kernel, dp, seq, heads, scale), out_shap...  64.6 us
    unnamed x19, local copies, waits for them, and re-layouts  7.26 us

profile of v1, /device:TPU:0, one launch (start us, length us, event | category | flops | bytes accessed | tf_op | source)
XLA Modules:
  0.0 72.6 jit_solution(15586583260179559904)
XLA Ops:
  0.6 0.0 copy-start.3
  0.6 0.0 copy-start.4
  0.7 0.0 copy-start.5
  0.7 0.0 copy-start.6
  0.7 0.9 %copy.12.wdt_ref = bf16[320,40]{1,0:T(8,128)(2,1)S(1)} copy(bf16[320,40]{0,1:T(8,128)(2,1)} %param.12) | data formatting | bytes 51200 | tf_op args[4]
  1.6 0.0 copy-done.3
  1.6 0.0 copy-done.4
  1.6 0.0 copy-done.5
  1.6 0.0 copy-done.6
  1.6 0.0 copy-start
  1.6 1.1 %copy-done = bf16[1,128,2560]{2,1,0:T(8,128)(2,1)S(1)} copy-done((bf16[1,128,2560]{2,1,0:T(8,128)(2,1)S(1)}, bf16[1,128,2560]{2,1,0:T(8,128)(2,1)}, u32[]{:S(2)}) %copy-start) | copy-done | bytes 655384
  2.7 0.0 copy-start.1
  2.7 1.1 %copy-done.1 = bf16[1,128,2560]{2,1,0:T(8,128)(2,1)S(1)} copy-done((bf16[1,128,2560]{2,1,0:T(8,128)(2,1)S(1)}, bf16[1,128,2560]{2,1,0:T(8,128)(2,1)}, u32[]{:S(2)}) %copy-start.1) | copy-done | bytes 655384
  3.8 0.0 copy-start.2
  3.8 1.1 %copy-done.2 = bf16[1,128,2560]{2,1,0:T(8,128)(2,1)S(1)} copy-done((bf16[1,128,2560]{2,1,0:T(8,128)(2,1)S(1)}, bf16[1,128,2560]{2,1,0:T(8,128)(2,1)}, u32[]{:S(2)}) %copy-start.2) | copy-done | bytes 655384
  4.9 64.6 %mixer_backward.1 = (bf16[128,2560]{1,0:T(8,128)(2,1)S(1)}, bf16[128,2560]{1,0:T(8,128)(2,1)S(1)}, f32[320,128]{1,0:T(8,128)S(1)}, f32[320,40]{1,0:T(8,128)S(1)}) custom-call(bf16[128,2560]{1,0:T(8,128)(2,1)S(1)} %bitcast.8, bf16[128,2560]{1,0:T(8,128)(2,1)S(1)} %bitcast.9, bf16[128,2560]{1,0:T(8,128)(2,1)S(1)} %bitcast.10, bf16[320,128]{1,0:T(8,128)(2,1)S(1)} %copy-done.3, ...), custom_call_target="tpu_custom_call" | custom-call | tf_op jit(solution)/shard_map/mixer_backward/pallas_call | solution.py:455
  69.5 0.7 %copy.13 = f32[320,40]{0,1:T(8,128)} copy(f32[320,40]{1,0:T(8,128)S(1)} %get-tuple-element.15) | data formatting | bytes 102400
  70.3 0.8 %copy.17 = bf16[1,128,2560]{2,1,0:T(8,128)(2,1)} copy(bf16[1,128,2560]{2,1,0:T(8,128)(2,1)S(1)} %bitcast.12) | data formatting | bytes 1310720
  71.1 0.8 %copy.18 = bf16[1,128,2560]{2,1,0:T(8,128)(2,1)} copy(bf16[1,128,2560]{2,1,0:T(8,128)(2,1)S(1)} %bitcast.11) | data formatting | bytes 1310720
  71.9 0.7 copy.19
Async XLA Ops:
  0.6 1.0 %copy-start.3 = (bf16[320,128]{1,0:T(8,128)(2,1)S(1)}, bf16[320,128]{1,0:T(8,128)(2,1)}, u32[]{:S(2)}) copy-start(bf16[320,128]{1,0:T(8,128)(2,1)} %wbc_ref.1) | copy-start | bytes 245764
  0.6 1.0 %copy-start.4 = (f32[40]{0:T(128)S(1)}, f32[40]{0:T(128)}, u32[]{:S(2)}) copy-start(f32[40]{0:T(128)} %param.13) | copy-start | bytes 484
  0.7 1.0 %copy-start.5 = (f32[40]{0:T(128)S(1)}, f32[40]{0:T(128)}, u32[]{:S(2)}) copy-start(f32[40]{0:T(128)} %param.14) | copy-start | bytes 484
  0.7 1.0 %copy-start.6 = (f32[40]{0:T(128)S(1)}, f32[40]{0:T(128)}, u32[]{:S(2)}) copy-start(f32[40]{0:T(128)} %param.15) | copy-start | bytes 484
  1.6 1.1 %copy-start = (bf16[1,128,2560]{2,1,0:T(8,128)(2,1)S(1)}, bf16[1,128,2560]{2,1,0:T(8,128)(2,1)}, u32[]{:S(2)}) copy-start(bf16[1,128,2560]{2,1,0:T(8,128)(2,1)} %param.8) | copy-start | bytes 1966084
  2.7 1.1 %copy-start.1 = (bf16[1,128,2560]{2,1,0:T(8,128)(2,1)S(1)}, bf16[1,128,2560]{2,1,0:T(8,128)(2,1)}, u32[]{:S(2)}) copy-start(bf16[1,128,2560]{2,1,0:T(8,128)(2,1)} %param.9) | copy-start | bytes 1966084
  3.8 1.1 %copy-start.2 = (bf16[1,128,2560]{2,1,0:T(8,128)(2,1)S(1)}, bf16[1,128,2560]{2,1,0:T(8,128)(2,1)}, u32[]{:S(2)}) copy-start(bf16[1,128,2560]{2,1,0:T(8,128)(2,1)} %param.10) | copy-start | bytes 1966084

commit v2 on v1

--- a/solution.py
+++ b/solution.py
@@ -34,8 +34,9 @@
 
 def kernel(
     dp, seq, heads, scale,
-    f_ref, x_ref, g_ref, wbc_ref, wdt_ref, bias_ref, decay_ref, skip_ref,
+    f_hbm, x_hbm, g_hbm, wbc_ref, wdt_ref, bias_ref, decay_ref, skip_ref,
     ig_ref, hg_ref, bcg_ref, dtg_ref, *,
+    f_ref, x_ref, g_ref, in_sem, ft_s, m_s, cum_w,
     wall, par, pre_s, step_s, cum_s, cumt_s, ecum_s, toend_s, proj_s, bct_s, inter_s, rows_s,
     ig_acc, step_w, ecum_w, toend_w, end_w, wgrad, sgrad, left_s, right_s,
     fin, bin_, fout, bout, red_s, bg_s, cg_s, gp_s,
@@ -48,6 +49,7 @@
     half = dp // 2
     sib = me + 1 - 2 * lax.rem(me, 2)
     length, inner = x_ref.shape
+    width = f_ref.shape[1]
     rows = wbc_ref.shape[0]
     state = wbc_ref.shape[1] // 2
     head_size = inner // heads
@@ -64,6 +66,12 @@
     def source(k):
         return lax.rem(me + dp - 2 * k, dp)
 
+    loads = [
+        pltpu.make_async_copy(src, dst, in_sem.at[i])
+        for i, (src, dst) in enumerate(((x_hbm, x_ref), (g_hbm, g_ref), (f_hbm, f_ref)))
+    ]
+    for load in loads:
+        load.start()
     barrier = pltpu.get_barrier_semaphore()
     pl.semaphore_signal(barrier, inc=1, device_id=at_dp(sib), device_id_type=MESH)
     for k in range(1, half):
@@ -75,10 +83,13 @@
         return pl.ds(pl.multiple_of(index * rows, 16), rows)
 
     wall[block(me), 0:LANES] = wbc_ref[...]
+    padded = -(-rows // LANES) * LANES
     wide = jnp.concatenate(
-        [wdt_ref[...].astype(F32), jnp.zeros((rows, LANES - heads), F32)], axis=1
+        [wdt_ref[...].astype(F32), jnp.zeros((LANES - heads, rows), F32)], axis=0
     )
-    wall[block(me), LANES:] = wide.astype(BF16)
+    if padded > rows:
+        wide = jnp.concatenate([wide, jnp.zeros((LANES, padded - rows), F32)], axis=1)
+    wall[block(me), LANES:] = wide.T[0:rows, :].astype(BF16)
     par[...] = jnp.zeros_like(par)
     par[0:1, 0:heads] = bias_ref[...]
     par[1:2, 0:heads] = decay_ref[...]
@@ -102,7 +113,28 @@
     for k in range(1, half):
         ag_copy(k, me, peer(k)).start()
     ag_copy(0, me, sib).start()
+    for load in loads:
+        load.wait()
+
+    low_half = iota((length, LANES), 1) < head_size
+    per_tile = LANES // head_size
+    tile_count = inner // LANES
+
+    def early_work(tile):
+        ts = pl.ds(pl.multiple_of(tile * LANES, LANES), LANES)
+        x_tile, g_full = x_ref[:, ts].astype(F32), g_ref[:, ts]
+        for part in range(per_tile):
+            mine = low_half if part == 0 else jnp.logical_not(low_half)
+            x_part = jnp.where(mine, x_tile, 0.0).astype(BF16)
+            m_s[tile * per_tile + part] = mm(x_part, g_full, NT)
+
+    @pl.loop(0, width // CHUNK)
+    def _(c):
+        cs = pl.ds(pl.multiple_of(c * CHUNK, CHUNK), CHUNK)
+        ft_s[cs, :] = f_ref[:, cs].T
+
     for k in range(1, half):
+        pl.loop(tile_count * (k - 1) // (half - 1), tile_count * k // (half - 1))(early_work)
         ag_copy(k, source(k), peer(k)).wait_recv()
         fw_copy(k, source(k)).start()
     ag_copy(0, sib, sib).wait_recv()
@@ -134,15 +166,28 @@
     c_rows = proj_s[:, state:]
     inter_s[...] = jnp.dot(b_rows, ct, precision=HIGHEST, preferred_element_type=F32)
 
-    def spread(value, c):
+    def spread(value, c, exact=False):
         high, low = halves(value)
         row = iota((LANES, CHUNK), 0)
         hot = (row == c * (CHUNK // head_size) + iota((LANES, CHUNK), 1) // head_size)
         hot = hot.astype(F32).astype(BF16)
-        return mm(jnp.concatenate([high, low], axis=1), jnp.concatenate([hot, hot], axis=0))
+        result = mm(jnp.concatenate([high, low], axis=1), jnp.concatenate([hot, hot], axis=0))
+        if exact:
+            rest = value - high.astype(F32) - low.astype(F32)
+            result = result + mm(rest.astype(BF16), hot)
+        return result
 
     def lanes(c):
         return pl.ds(pl.multiple_of(c * CHUNK, CHUNK), CHUNK)
+
+    def chain_copy(way, c):
+        src, dst = ((fout, fin), (bout, bin_))[way]
+        to = (z + 1, z + last)[way]
+        return pltpu.make_async_remote_copy(
+            src_ref=src.at[c], dst_ref=dst.at[c],
+            send_sem=ch_send.at[way, c], recv_sem=ch_recv.at[way, c],
+            device_id=(me, lax.rem(to, seq)), device_id_type=MESH,
+        )
 
     @pl.loop(0, chunks)
     def _(c):
@@ -155,6 +200,7 @@
         step_w[:, cs] = step_c
         ecum_w[:, cs] = ecum_c
         toend_w[:, cs] = toend_c
+        cum_w[:, cs] = spread(cum_s[...], c, exact=True)
         end_w[:, cs] = ends
         wgrad[:, cs] = weighted
         e_hi, e_lo = halves(ends)
@@ -162,62 +208,48 @@
         left_s[c] = mm(bt3, jnp.concatenate([e_hi, e_hi, e_lo], axis=0))
         right_s[c] = mm(ct3, jnp.concatenate([w_hi, w_hi, w_lo], axis=0))
 
-    def chain_copy(way, c):
-        src, dst = ((fout, fin), (bout, bin_))[way]
-        to = (z + 1, z + last)[way]
-        return pltpu.make_async_remote_copy(
-            src_ref=src.at[c], dst_ref=dst.at[c],
-            send_sem=ch_send.at[way, c], recv_sem=ch_recv.at[way, c],
-            device_id=(me, lax.rem(to, seq)), device_id_type=MESH,
-        )
+        for way, first in ((0, 0), (1, last)):
+            @pl.when(z == first)
+            def _():
+                arrived, leaving, here = ((fin, fout, left_s), (bin_, bout, right_s))[way]
+                arrived[c] = jnp.zeros((state, CHUNK), BF16)
+                if seq > 1:
+                    leaving[c] = here[c].astype(BF16)
+                    chain_copy(way, c).start()
 
     def chain_hop(way, c):
         arrived, leaving, local = ((fin, fout, left_s), (bin_, bout, right_s))[way]
-        first, final_one = ((0, last), (last, 0))[way]
-
-        @pl.when(z == first)
-        def _():
-            arrived[c] = jnp.zeros((state, CHUNK), arrived.dtype)
-            if seq > 1:
-                leaving[c] = local[c].astype(leaving.dtype)
-                chain_copy(way, c).start()
-
-        @pl.when(z != first)
-        def _():
-            chain_copy(way, c).wait_recv()
-
-            @pl.when(z != final_one)
-            def _():
-                decay = ecum_w[length - 1 :, lanes(c)]
-                leaving[c] = (arrived[c].astype(F32) * decay + local[c]).astype(leaving.dtype)
-                chain_copy(way, c).start()
+        chain_copy(way, c).wait_recv()
+
+        @pl.when(z != (last, 0)[way])
+        def _():
+            decay = ecum_w[length - 1 :, lanes(c)]
+            leaving[c] = (arrived[c].astype(F32) * decay + local[c]).astype(BF16)
+            chain_copy(way, c).start()
 
     later = iota((length, length), 1) >= iota((length, length), 0)
-    low_half = iota((length, LANES), 1) < head_size
-    per_tile = LANES // head_size
+    def by_head(tile):
+        turned = pltpu.roll(tile, head_size, 1)
+        return jnp.where(low_half, tile, turned), jnp.where(low_half, turned, tile)
 
     def tile_work(tile):
         ts = pl.ds(pl.multiple_of(tile * LANES, LANES), LANES)
-        x_tile, g_tile = x_ref[:, ts].astype(F32), g_ref[:, ts].astype(F32)
-        g_full = g_ref[:, ts]
-        step, cum, inter = step_s[...], cum_s[...], inter_s[...]
-        mixes, grads = [], []
+        g_tile = g_ref[:, ts].astype(F32)
+        inter = inter_s[...]
+        cums, steps = by_head(cum_w[:, ts]), by_head(step_w[:, ts])
+        mixes, grads, sums = [], [], []
         for part in range(per_tile):
             head = tile * per_tile + part
-            pick = iota((length, LANES), 1) == head
-            cum_col = jnp.sum(jnp.where(pick, cum, 0.0), axis=1, keepdims=True)
-            step_col = jnp.sum(jnp.where(pick, step, 0.0), axis=1, keepdims=True)
-            gap = cumt_s[pl.ds(head, 1), :] - cum_col
+            gap = cumt_s[pl.ds(head, 1), :] - cums[part]
             weights = jnp.exp(jnp.where(later, gap, -1e30))
             mine = low_half if part == 0 else jnp.logical_not(low_half)
-            x_part = jnp.where(mine, x_tile, 0.0).astype(BF16)
             g_part = jnp.where(mine, g_tile, 0.0).astype(BF16)
-            mixing_grad = mm(x_part, g_full, NT) * step_col
-            shared = mixing_grad * weights
-            ig_acc[...] += shared
+            shared = m_s[head] * steps[part] * weights
+            sums.append(shared)
             rows_s[pl.ds(head, 1), :] = jnp.sum(shared * inter, axis=0, keepdims=True)
             mixes += list(halves(inter * weights))
             grads += [g_part, g_part]
+        ig_acc[...] += sum(sums[1:], sums[0])
         sgrad[:, ts] = mm(jnp.concatenate(mixes, axis=1), jnp.concatenate(grads, axis=0))
 
     def reduce_heads(value, c):
@@ -263,24 +295,32 @@
     red_s[...] = jnp.zeros_like(red_s)
     tiles = CHUNK // LANES
 
-    @pl.loop(0, chunks + last)
+    early = tiles // 2
+
+    @pl.loop(0, chunks + max(last - 1, 0))
     def _(s):
-        forward, back = s - z, s - (last - z)
-
-        @pl.when(jnp.logical_and(forward >= 0, forward < chunks))
-        def _():
-            chain_hop(0, forward)
-
-        @pl.when(jnp.logical_and(back >= 0, back < chunks))
-        def _():
-            chain_hop(1, back)
+        forward, back = s - (z - 1), s - (last - 1 - z)
 
         @pl.when(s < chunks)
         def _():
-            for tile in range(tiles):
+            for tile in range(early):
                 tile_work(s * tiles + tile)
 
-        both = s - jnp.maximum(z, last - z)
+        if seq > 1:
+            @pl.when(jnp.logical_and(z > 0, jnp.logical_and(forward >= 0, forward < chunks)))
+            def _():
+                chain_hop(0, forward)
+
+            @pl.when(jnp.logical_and(z < last, jnp.logical_and(back >= 0, back < chunks)))
+            def _():
+                chain_hop(1, back)
+
+        @pl.when(s < chunks)
+        def _():
+            for tile in range(early, tiles):
+                tile_work(s * tiles + tile)
+
+        both = s - jnp.maximum(z, last - z) + min(last, 1)
 
         @pl.when(jnp.logical_and(both >= 0, both < chunks))
         def _():
@@ -304,10 +344,12 @@
     gp_s[:, LANES:] = pre_grad.astype(BF16)
     gproj = gp_s[...]
 
-    for c in range(chunks):
-        part = mm(f_ref[:, c * CHUNK : (c + 1) * CHUNK], gproj, TN)
-        gw[c * CHUNK : (c + 1) * CHUNK, :] = part
-        gw_out[c * CHUNK : (c + 1) * CHUNK, :] = part.astype(BF16)
+    @pl.loop(0, width // CHUNK)
+    def _(c):
+        cs = pl.ds(pl.multiple_of(c * CHUNK, CHUNK), CHUNK)
+        part = mm(ft_s[cs, :], gproj)
+        gw[cs, :] = part
+        gw_out[cs, :] = part.astype(BF16)
 
     def r1_copy(k, owner):
         return pltpu.make_async_remote_copy(
@@ -331,7 +373,7 @@
         s_out[k] = (gw[block(peer(k)), :] + rb1[k].astype(F32)).astype(BF16)
         r2_copy(k, peer(k)).start()
 
-    for c in range(chunks):
+    for c in range(width // CHUNK):
         cs = slice(c * CHUNK, (c + 1) * CHUNK)
         ig_ref[:, cs] = mm(gproj, wall[cs, :], NT).astype(BF16)
 
@@ -378,7 +420,7 @@
         for k in range(1, seq):
             zr_copy(k).wait_recv()
             mine = mine + zin[k].astype(F32)
-        final[z_piece(z), :] = mine * scale
+        final[z_piece(z), :] = (mine * scale).astype(BF16)
         for k in range(1, seq):
             za_copy(k, z).start()
 
@@ -387,8 +429,11 @@
         def _():
             za_copy(k, from_z(k)).wait_recv()
 
-    bcg_ref[...] = final[:, 0:LANES]
-    dtg_ref[...] = final[:, LANES : LANES + heads]
+    bcg_ref[...] = final[:, 0:LANES].astype(F32)
+    tail = final[:, LANES:].astype(F32)
+    if padded > rows:
+        tail = jnp.concatenate([tail, jnp.zeros((padded - rows, LANES), F32)], axis=0)
+    dtg_ref[...] = tail.T[0:heads, 0:rows]
 
     ag_copy(0, me, sib).wait_send()
     for k in range(1, half):
@@ -432,6 +477,10 @@
     wire = vmem((chunks, state, CHUNK), BF16)
     narrow = vmem((length, state), F32)
     scratch = dict(
+        f_ref=vmem((length, width), BF16), x_ref=vmem((length, inner), BF16),
+        g_ref=vmem((length, inner), BF16), in_sem=dma((3,)),
+        ft_s=vmem((width, length), BF16), m_s=vmem((heads, length, length), F32),
+        cum_w=broad,
         wall=vmem((width, 2 * LANES), BF16), par=vmem((8, LANES), F32),
         pre_s=square, step_s=square, cum_s=square, cumt_s=square, ecum_s=square,
         toend_s=square, proj_s=square, bct_s=square, inter_s=square, rows_s=square,
@@ -445,7 +494,7 @@
         rb1=vmem((half, rows, 2 * LANES), BF16), s_out=vmem((half, rows, 2 * LANES), BF16),
         rb2=vmem((half, rows, 2 * LANES), BF16),
         zout=vmem((rows, 2 * LANES), BF16), zin=vmem((seq, piece, 2 * LANES), BF16),
-        final=vmem((rows, 2 * LANES), F32),
+        final=vmem((rows, 2 * LANES), BF16),
         ag_send=dma((half,)), ag_recv=dma((half,)), fw_send=dma((half,)), fw_recv=dma((half,)),
         ch_send=dma((2, chunks)), ch_recv=dma((2, chunks)),
         r1_send=dma((half,)), r1_recv=dma((half,)), r2_send=dma((half,)), r2_recv=dma((half,)),
@@ -458,21 +507,21 @@
             jax.ShapeDtypeStruct((length, width), BF16),
             jax.ShapeDtypeStruct((length, inner), BF16),
             jax.ShapeDtypeStruct((rows, both), F32),
-            jax.ShapeDtypeStruct((rows, heads), F32),
+            jax.ShapeDtypeStruct((heads, rows), F32),
         ),
-        in_specs=[whole] * 8,
+        in_specs=[pl.BlockSpec(memory_space=pltpu.HBM)] * 3 + [whole] * 5,
         out_specs=(whole,) * 4,
         scratch_shapes=scratch,
         compiler_params=pltpu.CompilerParams(
-            collective_id=0, has_side_effects=True, vmem_limit_bytes=48 * 2**20
+            collective_id=0, has_side_effects=True, vmem_limit_bytes=56 * 2**20
         ),
         name="mixer_backward",
     )(
-        features[0], head_inputs[0], out_grad[0], bc_weight, dt_weight,
+        features[0], head_inputs[0], out_grad[0], bc_weight, dt_weight.T,
         dt_bias[None, :], decay_rate[None, :], skip_gain[None, :],
     )
     input_grad, head_grad, bc_grad, dt_grad = results
-    return input_grad[None], head_grad[None], bc_grad, dt_grad
+    return input_grad[None], head_grad[None], bc_grad, dt_grad.T
 
 
 def solution(mesh):

time: 72.9 us -> 67.5 us (0.926)
  local copies, waits for them, and re-layouts: 7.26 us -> 4.57 us
  Pallas kernels: 64.6 us -> 62 us
    unnamed x19 -> x10, local copies, waits for them, and re-layouts: 7.26 us -> 4.57 us
    pallas_call x1, Pallas kernels: 64.6 us -> 62 us  [body(): pl.pallas_call(functools.partial(kernel, dp, seq, heads, scale), out_shap...]
where the time goes in v2:
time: 67.5 us; the launch traced here: 67.2 us
  Pallas kernels  62 us (92%)
  local copies, waits for them, and re-layouts  4.57 us (7%)
    pallas_call x1, Pallas kernels, body(): pl.pallas_call(functools.partial(kernel, dp, seq, heads, scale), out_shap...  62 us
    unnamed x10, local copies, waits for them, and re-layouts  4.57 us

profile of v2, /device:TPU:0, one launch (start us, length us, event | category | flops | bytes accessed | tf_op | source)
XLA Modules:
  0.0 67.2 jit_solution(5530885992946487341)
XLA Ops:
  0.6 62.0 %mixer_backward.1 = (bf16[128,2560]{1,0:T(8,128)(2,1)}, bf16[128,2560]{1,0:T(8,128)(2,1)}, f32[320,128]{1,0:T(8,128)}, f32[40,320]{1,0:T(8,128)}) custom-call(bf16[128,2560]{1,0:T(8,128)(2,1)} %bitcast.10, bf16[128,2560]{1,0:T(8,128)(2,1)} %bitcast.11, bf16[128,2560]{1,0:T(8,128)(2,1)} %bitcast.12, bf16[320,128]{1,0:T(8,128)(2,1)} %wbc_ref.1, ...), custom_call_target="tpu_custom_call" | custom-call | tf_op jit(solution)/shard_map/mixer_backward/pallas_call | solution.py:504
  62.6 0.0 copy-start
  62.6 2.0 %copy.16 = bf16[1,128,2560]{2,1,0:T(8,128)(2,1)} copy(bf16[1,128,2560]{2,1,0:T(8,128)(2,1)} %bitcast.14) | data formatting | bytes 1310720
  64.7 0.0 copy-done
  64.7 0.0 copy-start.1
  64.7 0.8 %copy.17 = bf16[1,128,2560]{2,1,0:T(8,128)(2,1)} copy(bf16[1,128,2560]{2,1,0:T(8,128)(2,1)S(1)} %bitcast.13) | data formatting | bytes 1310720
  65.5 0.2 copy-done.1
  65.7 0.0 copy-start.2
  65.7 0.7 copy.18
  66.4 0.2 copy-done.2
  66.6 0.6 copy.19
Async XLA Ops:
  62.6 2.0 %copy-start = (bf16[128,2560]{1,0:T(8,128)(2,1)S(1)}, bf16[128,2560]{1,0:T(8,128)(2,1)}, u32[]{:S(2)}) copy-start(bf16[128,2560]{1,0:T(8,128)(2,1)} %get-tuple-element.9) | copy-start | bytes 1966084
  64.7 1.1 %copy-start.1 = (f32[320,128]{1,0:T(8,128)S(1)}, f32[320,128]{1,0:T(8,128)}, u32[]{:S(2)}) copy-start(f32[320,128]{1,0:T(8,128)} %get-tuple-element.18) | copy-start | bytes 491524
  65.7 0.9 %copy-start.2 = (f32[40,320]{1,0:T(8,128)S(1)}, f32[40,320]{1,0:T(8,128)}, u32[]{:S(2)}) copy-start(f32[40,320]{1,0:T(8,128)} %get-tuple-element.11) | copy-start | bytes 153604

commit v3 on v2

--- a/solution.py
+++ b/solution.py
@@ -35,14 +35,15 @@
 def kernel(
     dp, seq, heads, scale,
     f_hbm, x_hbm, g_hbm, wbc_ref, wdt_ref, bias_ref, decay_ref, skip_ref,
-    ig_ref, hg_ref, bcg_ref, dtg_ref, *,
-    f_ref, x_ref, g_ref, in_sem, ft_s, m_s, cum_w,
+    ig_hbm, hg_hbm, bcg_ref, dtg_ref, *,
+    ig_ref, hg_ref, out_sem,
+    f_ref, x_ref, g_ref, in_sem, ft_s, m_s, cum_w, hot_s, wpack, ftin, gpin, fa_send, fa_recv,
     wall, par, pre_s, step_s, cum_s, cumt_s, ecum_s, toend_s, proj_s, bct_s, inter_s, rows_s,
     ig_acc, step_w, ecum_w, toend_w, end_w, wgrad, sgrad, left_s, right_s,
-    fin, bin_, fout, bout, red_s, bg_s, cg_s, gp_s,
-    gw, gw_out, rb1, s_out, rb2, zout, zin, final,
+    fin, bin_, fout, bout, red_s, bg_s, cg_s,
+    zout, zin, final,
     ag_send, ag_recv, fw_send, fw_recv, ch_send, ch_recv,
-    r1_send, r1_recv, r2_send, r2_recv, zr_send, zr_recv, za_send, za_recv,
+    gp_send, gp_recv, gf_send, gf_recv, zr_send, zr_recv, za_send, za_recv,
 ):
     me, z = lax.axis_index("dp"), lax.axis_index("seq")
     last = seq - 1
@@ -54,8 +55,28 @@
     state = wbc_ref.shape[1] // 2
     head_size = inner // heads
     chunks = inner // CHUNK
-    piece = -(-rows // (16 * seq)) * 16
-    owners = -(-rows // piece)
+    groups = LANES // heads
+    share = -(-rows // (16 * groups)) * 16
+    packed = rows + share
+    piece = -(-packed // (16 * seq)) * 16
+    owners = -(-packed // piece)
+
+    def pack(value):
+        parts = []
+        for g in range(groups):
+            part = value[g * share : min((g + 1) * share, rows), :]
+            if part.shape[0] < share:
+                empty = jnp.zeros((share - part.shape[0], LANES), F32)
+                part = jnp.concatenate([part, empty], axis=0)
+            parts.append(pltpu.roll(part, g * heads, 1) if g else part)
+        return sum(parts[1:], parts[0])
+
+    def unpack(value):
+        parts = []
+        for g in range(groups):
+            part = pltpu.roll(value, LANES - g * heads, 1) if g else value
+            parts.append(part[0 : min(share, rows - g * share), :])
+        return jnp.concatenate(parts, axis=0)
 
     def at_dp(target):
         return (target, z)
@@ -73,39 +94,40 @@
     for load in loads:
         load.start()
     barrier = pltpu.get_barrier_semaphore()
-    pl.semaphore_signal(barrier, inc=1, device_id=at_dp(sib), device_id_type=MESH)
-    for k in range(1, half):
-        pl.semaphore_signal(barrier, inc=1, device_id=at_dp(peer(k)), device_id_type=MESH)
+    for k in range(1, dp):
+        pl.semaphore_signal(
+            barrier, inc=1, device_id=at_dp(lax.rem(me + k, dp)), device_id_type=MESH
+        )
     for k in range(1, seq):
         pl.semaphore_signal(barrier, inc=1, device_id=(me, lax.rem(z + k, seq)), device_id_type=MESH)
 
     def block(index):
         return pl.ds(pl.multiple_of(index * rows, 16), rows)
 
-    wall[block(me), 0:LANES] = wbc_ref[...]
+    wpack[me, 0:rows, :] = wbc_ref[...]
     padded = -(-rows // LANES) * LANES
     wide = jnp.concatenate(
         [wdt_ref[...].astype(F32), jnp.zeros((LANES - heads, rows), F32)], axis=0
     )
     if padded > rows:
         wide = jnp.concatenate([wide, jnp.zeros((LANES, padded - rows), F32)], axis=1)
-    wall[block(me), LANES:] = wide.T[0:rows, :].astype(BF16)
+    wpack[me, rows:, :] = pack(wide.T[0:rows, :]).astype(BF16)
     par[...] = jnp.zeros_like(par)
     par[0:1, 0:heads] = bias_ref[...]
     par[1:2, 0:heads] = decay_ref[...]
     par[2:3, 0:heads] = skip_ref[...]
-    pl.semaphore_wait(barrier, half + seq - 1)
+    pl.semaphore_wait(barrier, dp + seq - 2)
 
     def ag_copy(k, owner, target):
         return pltpu.make_async_remote_copy(
-            src_ref=wall.at[block(owner)], dst_ref=wall.at[block(owner)],
+            src_ref=wpack.at[owner], dst_ref=wpack.at[owner],
             send_sem=ag_send.at[k], recv_sem=ag_recv.at[k],
             device_id=at_dp(target), device_id_type=MESH,
         )
 
     def fw_copy(k, owner):
         return pltpu.make_async_remote_copy(
-            src_ref=wall.at[block(owner)], dst_ref=wall.at[block(owner)],
+            src_ref=wpack.at[owner], dst_ref=wpack.at[owner],
             send_sem=fw_send.at[k], recv_sem=fw_recv.at[k],
             device_id=at_dp(sib), device_id_type=MESH,
         )
@@ -133,6 +155,13 @@
         cs = pl.ds(pl.multiple_of(c * CHUNK, CHUNK), CHUNK)
         ft_s[cs, :] = f_ref[:, cs].T
 
+    @pl.loop(0, chunks)
+    def _(c):
+        lane = c * CHUNK + iota((LANES, CHUNK), 1)
+        hot = (iota((LANES, CHUNK), 0) == lane // head_size).astype(F32).astype(BF16)
+        hot_s[c, 0:LANES, :] = hot
+        hot_s[c, LANES:, :] = hot
+
     for k in range(1, half):
         pl.loop(tile_count * (k - 1) // (half - 1), tile_count * k // (half - 1))(early_work)
         ag_copy(k, source(k), peer(k)).wait_recv()
@@ -140,6 +169,23 @@
     ag_copy(0, sib, sib).wait_recv()
     for k in range(1, half):
         fw_copy(k, lax.rem(sib + dp - 2 * k, dp)).wait_recv()
+
+    def fa_copy(k):
+        target = lax.rem(me + k, dp)
+        return pltpu.make_async_remote_copy(
+            src_ref=ft_s.at[block(target)], dst_ref=ftin.at[me],
+            send_sem=fa_send.at[k], recv_sem=fa_recv.at[k],
+            device_id=at_dp(target), device_id_type=MESH,
+        )
+
+    for k in range(1, dp):
+        fa_copy(k).start()
+    ftin[me] = ft_s[block(me), :]
+
+    @pl.loop(0, dp)
+    def _(i):
+        wall[block(i), 0:LANES] = wpack[i, 0:rows, :]
+        wall[block(i), LANES:] = unpack(wpack[i, rows:, :].astype(F32)).astype(BF16)
 
     projection = mm(f_ref[...], wall[...])
     proj_s[...] = projection[:, :LANES]
@@ -168,13 +214,10 @@
 
     def spread(value, c, exact=False):
         high, low = halves(value)
-        row = iota((LANES, CHUNK), 0)
-        hot = (row == c * (CHUNK // head_size) + iota((LANES, CHUNK), 1) // head_size)
-        hot = hot.astype(F32).astype(BF16)
-        result = mm(jnp.concatenate([high, low], axis=1), jnp.concatenate([hot, hot], axis=0))
+        result = mm(jnp.concatenate([high, low], axis=1), hot_s[c])
         if exact:
             rest = value - high.astype(F32) - low.astype(F32)
-            result = result + mm(rest.astype(BF16), hot)
+            result = result + mm(rest.astype(BF16), hot_s[c, 0:LANES, :])
         return result
 
     def lanes(c):
@@ -253,11 +296,9 @@
         sgrad[:, ts] = mm(jnp.concatenate(mixes, axis=1), jnp.concatenate(grads, axis=0))
 
     def reduce_heads(value, c):
-        lane = iota((LANES, CHUNK), 0)
-        hot = lane == c * (CHUNK // head_size) + iota((LANES, CHUNK), 1) // head_size
-        hot = hot.astype(F32).astype(BF16)
+        hot = hot_s[c, 0:LANES, :]
         high, low = halves(value)
-        return mm(jnp.concatenate([high, low], axis=1), jnp.concatenate([hot, hot], axis=1), NT)
+        return mm(high, hot, NT) + mm(low, hot, NT)
 
     b_hi, b_lo = halves(b_rows)
     c_hi, c_lo = halves(c_rows)
@@ -326,6 +367,8 @@
         def _():
             carried_work(both)
 
+    store_hg = pltpu.make_async_copy(hg_ref, hg_hbm, out_sem.at[0])
+    store_hg.start()
     acc = ig_acc[...]
     c_grad = cg_s[...] + lax.dot_general(
         acc, b_rows, TN, precision=HIGHEST, preferred_element_type=F32
@@ -340,50 +383,56 @@
     decay_grad = jnp.dot(upper, cum_grad, precision=HIGHEST, preferred_element_type=F32)
     step_grad = direct - par[1:2, :] * decay_grad
     pre_grad = step_grad / (1.0 + jnp.exp(-pre_s[...]))
-    gp_s[:, 0:LANES] = jnp.concatenate([b_grad, c_grad], axis=1).astype(BF16)
-    gp_s[:, LANES:] = pre_grad.astype(BF16)
-    gproj = gp_s[...]
-
-    @pl.loop(0, width // CHUNK)
-    def _(c):
-        cs = pl.ds(pl.multiple_of(c * CHUNK, CHUNK), CHUNK)
-        part = mm(ft_s[cs, :], gproj)
-        gw[cs, :] = part
-        gw_out[cs, :] = part.astype(BF16)
-
-    def r1_copy(k, owner):
-        return pltpu.make_async_remote_copy(
-            src_ref=gw_out.at[block(owner)], dst_ref=rb1.at[k],
-            send_sem=r1_send.at[k], recv_sem=r1_recv.at[k],
+    gpin[me, :, 0:LANES] = jnp.concatenate([b_grad, c_grad], axis=1).astype(BF16)
+    gpin[me, :, LANES:] = pre_grad.astype(BF16)
+
+    def gp_copy(k, owner, target):
+        return pltpu.make_async_remote_copy(
+            src_ref=gpin.at[owner], dst_ref=gpin.at[owner],
+            send_sem=gp_send.at[k], recv_sem=gp_recv.at[k],
+            device_id=at_dp(target), device_id_type=MESH,
+        )
+
+    def gf_copy(k, owner):
+        return pltpu.make_async_remote_copy(
+            src_ref=gpin.at[owner], dst_ref=gpin.at[owner],
+            send_sem=gf_send.at[k], recv_sem=gf_recv.at[k],
             device_id=at_dp(sib), device_id_type=MESH,
         )
 
-    def r2_copy(k, target):
-        return pltpu.make_async_remote_copy(
-            src_ref=s_out.at[k], dst_ref=rb2.at[k],
-            send_sem=r2_send.at[k], recv_sem=r2_recv.at[k],
-            device_id=at_dp(target), device_id_type=MESH,
-        )
-
-    order = list(range(1, half)) + [0]
-    for k in order:
-        r1_copy(k, lax.rem(sib + 2 * k, dp)).start()
-    for k in order[:-1]:
-        r1_copy(k, sib).wait_recv()
-        s_out[k] = (gw[block(peer(k)), :] + rb1[k].astype(F32)).astype(BF16)
-        r2_copy(k, peer(k)).start()
-
+    for k in range(1, half):
+        gp_copy(k, me, peer(k)).start()
+    gp_copy(0, me, sib).start()
+
+    gproj = gpin[me]
     for c in range(width // CHUNK):
         cs = slice(c * CHUNK, (c + 1) * CHUNK)
         ig_ref[:, cs] = mm(gproj, wall[cs, :], NT).astype(BF16)
-
-    r1_copy(0, sib).wait_recv()
-    total = gw[block(me), :] + rb1[0].astype(F32)
+    store_ig = pltpu.make_async_copy(ig_ref, ig_hbm, out_sem.at[1])
+    store_ig.start()
+
+    for k in range(1, dp):
+        fa_copy(k).wait_recv()
+
+    def gradient_of(index):
+        return mm(ftin[index], gpin[index])
+
+    total = gradient_of(me)
+    gp_copy(0, sib, sib).wait_recv()
+    total = total + gradient_of(sib)
     for k in range(1, half):
-        r2_copy(k, peer(k)).wait_recv()
-        total = total + rb2[k].astype(F32)
-
-    zout[...] = total.astype(zout.dtype)
+        gp_copy(k, source(k), peer(k)).wait_recv()
+        gf_copy(k, source(k)).start()
+        total = total + gradient_of(source(k))
+    for k in range(1, half):
+        other = lax.rem(sib + dp - 2 * k, dp)
+        gf_copy(k, other).wait_recv()
+        total = total + gradient_of(other)
+
+    zout[0:rows, :] = total[:, 0:LANES].astype(BF16)
+    zout[rows:packed, :] = pack(total[:, LANES:]).astype(BF16)
+    if owners * piece > packed:
+        zout[packed:, :] = jnp.zeros((owners * piece - packed, LANES), BF16)
 
     def z_piece(index):
         return pl.ds(pl.multiple_of(index * piece, 16), piece)
@@ -429,19 +478,23 @@
         def _():
             za_copy(k, from_z(k)).wait_recv()
 
-    bcg_ref[...] = final[:, 0:LANES].astype(F32)
-    tail = final[:, LANES:].astype(F32)
+    bcg_ref[...] = final[0:rows, :].astype(F32)
+    tail = unpack(final[rows:packed, :].astype(F32))
     if padded > rows:
         tail = jnp.concatenate([tail, jnp.zeros((padded - rows, LANES), F32)], axis=0)
     dtg_ref[...] = tail.T[0:heads, 0:rows]
 
+    store_hg.wait()
+    store_ig.wait()
     ag_copy(0, me, sib).wait_send()
     for k in range(1, half):
         ag_copy(k, me, peer(k)).wait_send()
         fw_copy(k, source(k)).wait_send()
-        r2_copy(k, peer(k)).wait_send()
-    for k in range(half):
-        r1_copy(k, sib).wait_send()
+        gp_copy(k, me, peer(k)).wait_send()
+        gf_copy(k, source(k)).wait_send()
+    gp_copy(0, me, sib).wait_send()
+    for k in range(1, dp):
+        fa_copy(k).wait_send()
     for k in range(1, seq):
         @pl.when(to_z(k) < owners)
         def _():
@@ -458,6 +511,15 @@
             @pl.loop(0, chunks)
             def _(c):
                 chain_copy(way, c).wait_send()
+
+
+def place(*refs):
+    sem = refs[8]
+    copies = [pltpu.make_async_copy(refs[i], refs[i + 4], sem.at[i]) for i in range(4)]
+    for copy in copies:
+        copy.start()
+    for copy in copies:
+        copy.wait()
 
 
 def body(dp, seq, features, head_inputs, out_grad, bc_weight, dt_weight, dt_bias, decay_rate, skip_gain):
@@ -468,7 +530,10 @@
     state = both // 2
     half = dp // 2
     chunks = inner // CHUNK
-    piece = -(-rows // (16 * seq)) * 16
+    share = -(-rows // (16 * (LANES // heads))) * 16
+    packed = rows + share
+    piece = -(-packed // (16 * seq)) * 16
+    owners = -(-packed // piece)
     scale = 1.0 / math.sqrt(dp * seq * length)
     vmem, dma = pltpu.VMEM, pltpu.SemaphoreType.DMA
     square = vmem((length, LANES), F32)
@@ -479,6 +544,7 @@
     scratch = dict(
         f_ref=vmem((length, width), BF16), x_ref=vmem((length, inner), BF16),
         g_ref=vmem((length, inner), BF16), in_sem=dma((3,)),
+        ig_ref=vmem((length, width), BF16), hg_ref=vmem((length, inner), BF16), out_sem=dma((2,)),
         ft_s=vmem((width, length), BF16), m_s=vmem((heads, length, length), F32),
         cum_w=broad,
         wall=vmem((width, 2 * LANES), BF16), par=vmem((8, LANES), F32),
@@ -489,15 +555,14 @@
         left_s=states, right_s=states,
         fin=wire, bin_=wire, fout=wire, bout=wire,
         red_s=vmem((2 * length + 8, LANES), F32), bg_s=narrow, cg_s=narrow,
-        gp_s=vmem((length, 2 * LANES), BF16),
-        gw=vmem((width, 2 * LANES), F32), gw_out=vmem((width, 2 * LANES), BF16),
-        rb1=vmem((half, rows, 2 * LANES), BF16), s_out=vmem((half, rows, 2 * LANES), BF16),
-        rb2=vmem((half, rows, 2 * LANES), BF16),
-        zout=vmem((rows, 2 * LANES), BF16), zin=vmem((seq, piece, 2 * LANES), BF16),
-        final=vmem((rows, 2 * LANES), BF16),
+        hot_s=vmem((chunks, 2 * LANES, CHUNK), BF16), wpack=vmem((dp, packed, LANES), BF16),
+        ftin=vmem((dp, rows, length), BF16), gpin=vmem((dp, length, 2 * LANES), BF16),
+        fa_send=dma((dp,)), fa_recv=dma((dp,)),
+        zout=vmem((owners * piece, LANES), BF16), zin=vmem((seq, piece, LANES), BF16),
+        final=vmem((owners * piece, LANES), BF16),
         ag_send=dma((half,)), ag_recv=dma((half,)), fw_send=dma((half,)), fw_recv=dma((half,)),
         ch_send=dma((2, chunks)), ch_recv=dma((2, chunks)),
-        r1_send=dma((half,)), r1_recv=dma((half,)), r2_send=dma((half,)), r2_recv=dma((half,)),
+        gp_send=dma((half,)), gp_recv=dma((half,)), gf_send=dma((half,)), gf_recv=dma((half,)),
         zr_send=dma((seq,)), zr_recv=dma((seq,)), za_send=dma((seq,)), za_recv=dma((seq,)),
     )
     whole = pl.BlockSpec(memory_space=pltpu.VMEM)
@@ -510,7 +575,7 @@
             jax.ShapeDtypeStruct((heads, rows), F32),
         ),
         in_specs=[pl.BlockSpec(memory_space=pltpu.HBM)] * 3 + [whole] * 5,
-        out_specs=(whole,) * 4,
+        out_specs=(pl.BlockSpec(memory_space=pltpu.HBM),) * 2 + (whole,) * 2,
         scratch_shapes=scratch,
         compiler_params=pltpu.CompilerParams(
             collective_id=0, has_side_effects=True, vmem_limit_bytes=56 * 2**20
@@ -520,6 +585,15 @@
         features[0], head_inputs[0], out_grad[0], bc_weight, dt_weight.T,
         dt_bias[None, :], decay_rate[None, :], skip_gain[None, :],
     )
+    hbm = pl.BlockSpec(memory_space=pltpu.HBM)
+    results = pl.pallas_call(
+        place,
+        out_shape=tuple(jax.ShapeDtypeStruct(part.shape, part.dtype) for part in results),
+        in_specs=[pl.BlockSpec(memory_space=pl.ANY)] * 4,
+        out_specs=(hbm,) * 4,
+        scratch_shapes=[dma((4,))],
+        name="place_results",
+    )(*results)
     input_grad, head_grad, bc_grad, dt_grad = results
     return input_grad[None], head_grad[None], bc_grad, dt_grad.T
 

time: 67.5 us -> 104 us (1.54)
  Pallas kernels: 62 us -> 103 us
  local copies, waits for them, and re-layouts: 4.57 us -> 0 us
    pallas_call x0 -> x1, Pallas kernels: none -> 47.7 us  [body(): pl.pallas_call(place, out_shape=tuple((jax.ShapeDtypeStruct(part.shape, p...]
    pallas_call x1, Pallas kernels: 62 us -> 55.1 us  [body(): pl.pallas_call(functools.partial(kernel, dp, seq, heads, scale), out_shap...]
    unnamed x10 -> x0, local copies, waits for them, and re-layouts: 4.57 us -> none
where the time goes in v3:
time: 104 us; the launch traced here: 103 us
  Pallas kernels  103 us (99%)
    pallas_call x1, Pallas kernels, body(): pl.pallas_call(functools.partial(kernel, dp, seq, heads, scale), out_shap...  55.1 us
    pallas_call x1, Pallas kernels, body(): pl.pallas_call(place, out_shape=tuple((jax.ShapeDtypeStruct(part.shape, p...  47.7 us

profile of v3, /device:TPU:0, one launch (start us, length us, event | category | flops | bytes accessed | tf_op | source)
XLA Modules:
  0.0 103.4 jit_solution(10378368985069501566)
XLA Ops:
  0.6 55.1 %mixer_backward.1 = (bf16[128,2560]{1,0:T(8,128)(2,1)}, bf16[128,2560]{1,0:T(8,128)(2,1)}, f32[320,128]{1,0:T(8,128)}, f32[40,320]{1,0:T(8,128)}) custom-call(bf16[128,2560]{1,0:T(8,128)(2,1)} %bitcast.10, bf16[128,2560]{1,0:T(8,128)(2,1)} %bitcast.11, bf16[128,2560]{1,0:T(8,128)(2,1)} %bitcast.12, bf16[320,128]{1,0:T(8,128)(2,1)} %wbc_ref.1, ...), custom_call_target="tpu_custom_call" | custom-call | tf_op jit(solution)/shard_map/mixer_backward/pallas_call | solution.py:569
  55.7 47.7 %place_results.1 = (bf16[128,2560]{1,0:T(8,128)(2,1)}, bf16[128,2560]{1,0:T(8,128)(2,1)}, f32[320,128]{1,0:T(8,128)}, f32[40,320]{1,0:T(8,128)}) custom-call(bf16[128,2560]{1,0:T(8,128)(2,1)} %get-tuple-element.12.refs_0_, bf16[128,2560]{1,0:T(8,128)(2,1)} %get-tuple-element.13.refs_1_, f32[320,128]{1,0:T(8,128)} %get-tuple-element.14.refs_2_, ...), custom_call_target="tpu_custom_call" | custom-call | tf_op jit(solution)/shard_map/place_results/pallas_call | solution.py:589

commit v4 on v3

--- a/solution.py
+++ b/solution.py
@@ -11,7 +11,7 @@
 MESH = pl.DeviceIdType.MESH
 F32, BF16 = jnp.float32, jnp.bfloat16
 LANES = 128
-CHUNK = 512
+CHUNK = 256
 HIGHEST = lax.Precision.HIGHEST
 NT = (((1,), (1,)), ((), ()))
 TN = (((0,), (0,)), ((), ()))
@@ -514,12 +514,23 @@
 
 
 def place(*refs):
-    sem = refs[8]
-    copies = [pltpu.make_async_copy(refs[i], refs[i + 4], sem.at[i]) for i in range(4)]
-    for copy in copies:
-        copy.start()
-    for copy in copies:
-        copy.wait()
+    sources, targets, held, sem = refs[0:4], refs[4:8], refs[8:12], refs[12]
+    slots = []
+    for index, source in enumerate(sources):
+        parts = 4 if source.dtype == BF16 else 1
+        step = source.shape[0] // parts
+        slots += [(index, slice(part * step, (part + 1) * step)) for part in range(parts)]
+    loads, stores = [], []
+    for slot, (index, part) in enumerate(slots):
+        source, middle, target = sources[index].at[part], held[index].at[part], targets[index].at[part]
+        loads.append(pltpu.make_async_copy(source, middle, sem.at[0, slot]))
+        stores.append(pltpu.make_async_copy(middle, target, sem.at[1, slot]))
+        loads[-1].start()
+    for load, store in zip(loads, stores):
+        load.wait()
+        store.start()
+    for store in stores:
+        store.wait()
 
 
 def body(dp, seq, features, head_inputs, out_grad, bc_weight, dt_weight, dt_bias, decay_rate, skip_gain):
@@ -589,9 +600,9 @@
     results = pl.pallas_call(
         place,
         out_shape=tuple(jax.ShapeDtypeStruct(part.shape, part.dtype) for part in results),
-        in_specs=[pl.BlockSpec(memory_space=pl.ANY)] * 4,
+        in_specs=[hbm] * 4,
         out_specs=(hbm,) * 4,
-        scratch_shapes=[dma((4,))],
+        scratch_shapes=[vmem(part.shape, part.dtype) for part in results] + [dma((2, 10))],
         name="place_results",
     )(*results)
     input_grad, head_grad, bc_grad, dt_grad = results

time: 104 us -> 66.3 us (0.64)
  Pallas kernels: 103 us -> 65.5 us
    pallas_call x1, Pallas kernels: 47.7 us -> 2.31 us  [body(): pl.pallas_call(place, out_shape=tuple((jax.ShapeDtypeStruct(part.shape, p...]
    pallas_call x1, Pallas kernels: 55.1 us -> 63.2 us  [body(): pl.pallas_call(functools.partial(kernel, dp, seq, heads, scale), out_shap...]
where the time goes in v4:
time: 66.3 us; the launch traced here: 66.1 us
  Pallas kernels  65.5 us (99%)
    pallas_call x1, Pallas kernels, body(): pl.pallas_call(functools.partial(kernel, dp, seq, heads, scale), out_shap...  63.2 us
    pallas_call x1, Pallas kernels, body(): pl.pallas_call(place, out_shape=tuple((jax.ShapeDtypeStruct(part.shape, p...  2.31 us

profile of v4, /device:TPU:0, one launch (start us, length us, event | category | flops | bytes accessed | tf_op | source)
XLA Modules:
  0.0 66.1 jit_solution(12277087993977593661)
XLA Ops:
  0.6 63.2 %mixer_backward.1 = (bf16[128,2560]{1,0:T(8,128)(2,1)}, bf16[128,2560]{1,0:T(8,128)(2,1)}, f32[320,128]{1,0:T(8,128)}, f32[40,320]{1,0:T(8,128)}) custom-call(bf16[128,2560]{1,0:T(8,128)(2,1)} %bitcast.10, bf16[128,2560]{1,0:T(8,128)(2,1)} %bitcast.11, bf16[128,2560]{1,0:T(8,128)(2,1)} %bitcast.12, bf16[320,128]{1,0:T(8,128)(2,1)} %wbc_ref.1, ...), custom_call_target="tpu_custom_call" | custom-call | tf_op jit(solution)/shard_map/mixer_backward/pallas_call | solution.py:580
  63.8 2.3 %place_results.1 = (bf16[128,2560]{1,0:T(8,128)(2,1)}, bf16[128,2560]{1,0:T(8,128)(2,1)}, f32[320,128]{1,0:T(8,128)}, f32[40,320]{1,0:T(8,128)}) custom-call(bf16[128,2560]{1,0:T(8,128)(2,1)} %get-tuple-element.12.refs_0_, bf16[128,2560]{1,0:T(8,128)(2,1)} %get-tuple-element.13.refs_1_, f32[320,128]{1,0:T(8,128)} %get-tuple-element.14.refs_2_, ...), custom_call_target="tpu_custom_call" | custom-call | tf_op jit(solution)/shard_map/place_results/pallas_call | solution.py:600

commit v5 on v4

--- a/solution.py
+++ b/solution.py
@@ -11,7 +11,7 @@
 MESH = pl.DeviceIdType.MESH
 F32, BF16 = jnp.float32, jnp.bfloat16
 LANES = 128
-CHUNK = 256
+CHUNK = 512
 HIGHEST = lax.Precision.HIGHEST
 NT = (((1,), (1,)), ((), ()))
 TN = (((0,), (0,)), ((), ()))
@@ -61,21 +61,25 @@
     piece = -(-packed // (16 * seq)) * 16
     owners = -(-packed // piece)
 
-    def pack(value):
+    part_rows = -(-length // (16 * groups)) * 16
+
+    def pack(value, each):
+        value = jnp.where(iota(value.shape, 1) < heads, value, 0.0)
         parts = []
         for g in range(groups):
-            part = value[g * share : min((g + 1) * share, rows), :]
-            if part.shape[0] < share:
-                empty = jnp.zeros((share - part.shape[0], LANES), F32)
+            part = value[g * each : min((g + 1) * each, value.shape[0]), :]
+            if part.shape[0] < each:
+                empty = jnp.zeros((each - part.shape[0], LANES), F32)
                 part = jnp.concatenate([part, empty], axis=0)
             parts.append(pltpu.roll(part, g * heads, 1) if g else part)
         return sum(parts[1:], parts[0])
 
-    def unpack(value):
+    def unpack(value, count):
+        each = value.shape[0]
         parts = []
         for g in range(groups):
             part = pltpu.roll(value, LANES - g * heads, 1) if g else value
-            parts.append(part[0 : min(share, rows - g * share), :])
+            parts.append(part[0 : min(each, count - g * each), :])
         return jnp.concatenate(parts, axis=0)
 
     def at_dp(target):
@@ -111,7 +115,7 @@
     )
     if padded > rows:
         wide = jnp.concatenate([wide, jnp.zeros((LANES, padded - rows), F32)], axis=1)
-    wpack[me, rows:, :] = pack(wide.T[0:rows, :]).astype(BF16)
+    wpack[me, rows:, :] = pack(wide.T[0:rows, :], share).astype(BF16)
     par[...] = jnp.zeros_like(par)
     par[0:1, 0:heads] = bias_ref[...]
     par[1:2, 0:heads] = decay_ref[...]
@@ -143,7 +147,7 @@
     tile_count = inner // LANES
 
     def early_work(tile):
-        ts = pl.ds(pl.multiple_of(tile * LANES, LANES), LANES)
+        ts = slice(tile * LANES, (tile + 1) * LANES)
         x_tile, g_full = x_ref[:, ts].astype(F32), g_ref[:, ts]
         for part in range(per_tile):
             mine = low_half if part == 0 else jnp.logical_not(low_half)
@@ -163,7 +167,8 @@
         hot_s[c, LANES:, :] = hot
 
     for k in range(1, half):
-        pl.loop(tile_count * (k - 1) // (half - 1), tile_count * k // (half - 1))(early_work)
+        for tile in range(tile_count * (k - 1) // (half - 1), tile_count * k // (half - 1)):
+            early_work(tile)
         ag_copy(k, source(k), peer(k)).wait_recv()
         fw_copy(k, source(k)).start()
     ag_copy(0, sib, sib).wait_recv()
@@ -182,10 +187,10 @@
         fa_copy(k).start()
     ftin[me] = ft_s[block(me), :]
 
-    @pl.loop(0, dp)
+    @pl.loop(0, dp, unroll=4)
     def _(i):
         wall[block(i), 0:LANES] = wpack[i, 0:rows, :]
-        wall[block(i), LANES:] = unpack(wpack[i, rows:, :].astype(F32)).astype(BF16)
+        wall[block(i), LANES:] = unpack(wpack[i, rows:, :].astype(F32), rows).astype(BF16)
 
     projection = mm(f_ref[...], wall[...])
     proj_s[...] = projection[:, :LANES]
@@ -232,8 +237,7 @@
             device_id=(me, lax.rem(to, seq)), device_id_type=MESH,
         )
 
-    @pl.loop(0, chunks)
-    def _(c):
+    def local_work(c):
         cs = lanes(c)
         step_c = spread(step_s[...], c)
         ecum_c = spread(ecum_s[...], c)
@@ -251,6 +255,7 @@
         left_s[c] = mm(bt3, jnp.concatenate([e_hi, e_hi, e_lo], axis=0))
         right_s[c] = mm(ct3, jnp.concatenate([w_hi, w_hi, w_lo], axis=0))
 
+    def chain_start(c):
         for way, first in ((0, 0), (1, last)):
             @pl.when(z == first)
             def _():
@@ -336,7 +341,8 @@
     red_s[...] = jnp.zeros_like(red_s)
     tiles = CHUNK // LANES
 
-    early = tiles // 2
+    local_work(0)
+    chain_start(0)
 
     @pl.loop(0, chunks + max(last - 1, 0))
     def _(s):
@@ -344,8 +350,13 @@
 
         @pl.when(s < chunks)
         def _():
-            for tile in range(early):
+            local_work(jnp.minimum(s + 1, chunks - 1))
+            for tile in range(tiles):
                 tile_work(s * tiles + tile)
+
+        @pl.when(s < chunks - 1)
+        def _():
+            chain_start(s + 1)
 
         if seq > 1:
             @pl.when(jnp.logical_and(z > 0, jnp.logical_and(forward >= 0, forward < chunks)))
@@ -355,11 +366,6 @@
             @pl.when(jnp.logical_and(z < last, jnp.logical_and(back >= 0, back < chunks)))
             def _():
                 chain_hop(1, back)
-
-        @pl.when(s < chunks)
-        def _():
-            for tile in range(early, tiles):
-                tile_work(s * tiles + tile)
 
         both = s - jnp.maximum(z, last - z) + min(last, 1)
 
@@ -374,6 +380,30 @@
         acc, b_rows, TN, precision=HIGHEST, preferred_element_type=F32
     )
     b_grad = bg_s[...] + jnp.dot(acc, c_rows, precision=HIGHEST, preferred_element_type=F32)
+    pair = (pl.ds(0, length), pl.ds(length, part_rows))
+
+    def gp_copy(p, k, owner, target):
+        return pltpu.make_async_remote_copy(
+            src_ref=gpin.at[owner, pair[p]], dst_ref=gpin.at[owner, pair[p]],
+            send_sem=gp_send.at[p, k], recv_sem=gp_recv.at[p, k],
+            device_id=at_dp(target), device_id_type=MESH,
+        )
+
+    def gf_copy(p, k, owner):
+        return pltpu.make_async_remote_copy(
+            src_ref=gpin.at[owner, pair[p]], dst_ref=gpin.at[owner, pair[p]],
+            send_sem=gf_send.at[p, k], recv_sem=gf_recv.at[p, k],
+            device_id=at_dp(sib), device_id_type=MESH,
+        )
+
+    def gp_start(p):
+        for k in range(1, half):
+            gp_copy(p, k, me, peer(k)).start()
+        gp_copy(p, 0, me, sib).start()
+
+    state_part = jnp.concatenate([b_grad, c_grad], axis=1).astype(BF16)
+    gpin[me, 0:length, :] = state_part
+    gp_start(0)
     step = step_s[...]
     direct = red_s[length : 2 * length, :]
     cum_grad = rows_s[...].T + red_s[0:length, :] - step * direct
@@ -383,28 +413,9 @@
     decay_grad = jnp.dot(upper, cum_grad, precision=HIGHEST, preferred_element_type=F32)
     step_grad = direct - par[1:2, :] * decay_grad
     pre_grad = step_grad / (1.0 + jnp.exp(-pre_s[...]))
-    gpin[me, :, 0:LANES] = jnp.concatenate([b_grad, c_grad], axis=1).astype(BF16)
-    gpin[me, :, LANES:] = pre_grad.astype(BF16)
-
-    def gp_copy(k, owner, target):
-        return pltpu.make_async_remote_copy(
-            src_ref=gpin.at[owner], dst_ref=gpin.at[owner],
-            send_sem=gp_send.at[k], recv_sem=gp_recv.at[k],
-            device_id=at_dp(target), device_id_type=MESH,
-        )
-
-    def gf_copy(k, owner):
-        return pltpu.make_async_remote_copy(
-            src_ref=gpin.at[owner], dst_ref=gpin.at[owner],
-            send_sem=gf_send.at[k], recv_sem=gf_recv.at[k],
-            device_id=at_dp(sib), device_id_type=MESH,
-        )
-
-    for k in range(1, half):
-        gp_copy(k, me, peer(k)).start()
-    gp_copy(0, me, sib).start()
-
-    gproj = gpin[me]
+    gpin[me, length:, :] = pack(pre_grad, part_rows).astype(BF16)
+    gp_start(1)
+    gproj = jnp.concatenate([state_part, pre_grad.astype(BF16)], axis=1)
     for c in range(width // CHUNK):
         cs = slice(c * CHUNK, (c + 1) * CHUNK)
         ig_ref[:, cs] = mm(gproj, wall[cs, :], NT).astype(BF16)
@@ -415,22 +426,26 @@
         fa_copy(k).wait_recv()
 
     def gradient_of(index):
-        return mm(ftin[index], gpin[index])
-
-    total = gradient_of(me)
-    gp_copy(0, sib, sib).wait_recv()
+        steps = unpack(gpin[index, length:, :].astype(F32), length).astype(BF16)
+        return mm(ftin[index], jnp.concatenate([gpin[index, 0:length, :], steps], axis=1))
+
+    total = mm(ftin[me], gproj)
+    for k in range(1, half):
+        for p in range(2):
+            gp_copy(p, k, source(k), peer(k)).wait_recv()
+            gf_copy(p, k, source(k)).start()
+        total = total + gradient_of(source(k))
+    for p in range(2):
+        gp_copy(p, 0, sib, sib).wait_recv()
     total = total + gradient_of(sib)
     for k in range(1, half):
-        gp_copy(k, source(k), peer(k)).wait_recv()
-        gf_copy(k, source(k)).start()
-        total = total + gradient_of(source(k))
-    for k in range(1, half):
         other = lax.rem(sib + dp - 2 * k, dp)
-        gf_copy(k, other).wait_recv()
+        for p in range(2):
+            gf_copy(p, k, other).wait_recv()
         total = total + gradient_of(other)
 
     zout[0:rows, :] = total[:, 0:LANES].astype(BF16)
-    zout[rows:packed, :] = pack(total[:, LANES:]).astype(BF16)
+    zout[rows:packed, :] = pack(total[:, LANES:], share).astype(BF16)
     if owners * piece > packed:
         zout[packed:, :] = jnp.zeros((owners * piece - packed, LANES), BF16)
 
@@ -479,7 +494,7 @@
             za_copy(k, from_z(k)).wait_recv()
 
     bcg_ref[...] = final[0:rows, :].astype(F32)
-    tail = unpack(final[rows:packed, :].astype(F32))
+    tail = unpack(final[rows:packed, :].astype(F32), rows)
     if padded > rows:
         tail = jnp.concatenate([tail, jnp.zeros((padded - rows, LANES), F32)], axis=0)
     dtg_ref[...] = tail.T[0:heads, 0:rows]
@@ -490,9 +505,11 @@
     for k in range(1, half):
         ag_copy(k, me, peer(k)).wait_send()
         fw_copy(k, source(k)).wait_send()
-        gp_copy(k, me, peer(k)).wait_send()
-        gf_copy(k, source(k)).wait_send()
-    gp_copy(0, me, sib).wait_send()
+        for p in range(2):
+            gp_copy(p, k, me, peer(k)).wait_send()
+            gf_copy(p, k, source(k)).wait_send()
+    for p in range(2):
+        gp_copy(p, 0, me, sib).wait_send()
     for k in range(1, dp):
         fa_copy(k).wait_send()
     for k in range(1, seq):
@@ -542,6 +559,7 @@
     half = dp // 2
     chunks = inner // CHUNK
     share = -(-rows // (16 * (LANES // heads))) * 16
+    part_rows = -(-length // (16 * (LANES // heads))) * 16
     packed = rows + share
     piece = -(-packed // (16 * seq)) * 16
     owners = -(-packed // piece)
@@ -567,13 +585,14 @@
         fin=wire, bin_=wire, fout=wire, bout=wire,
         red_s=vmem((2 * length + 8, LANES), F32), bg_s=narrow, cg_s=narrow,
         hot_s=vmem((chunks, 2 * LANES, CHUNK), BF16), wpack=vmem((dp, packed, LANES), BF16),
-        ftin=vmem((dp, rows, length), BF16), gpin=vmem((dp, length, 2 * LANES), BF16),
+        ftin=vmem((dp, rows, length), BF16), gpin=vmem((dp, length + part_rows, LANES), BF16),
         fa_send=dma((dp,)), fa_recv=dma((dp,)),
         zout=vmem((owners * piece, LANES), BF16), zin=vmem((seq, piece, LANES), BF16),
         final=vmem((owners * piece, LANES), BF16),
         ag_send=dma((half,)), ag_recv=dma((half,)), fw_send=dma((half,)), fw_recv=dma((half,)),
         ch_send=dma((2, chunks)), ch_recv=dma((2, chunks)),
-        gp_send=dma((half,)), gp_recv=dma((half,)), gf_send=dma((half,)), gf_recv=dma((half,)),
+        gp_send=dma((2, half)), gp_recv=dma((2, half)),
+        gf_send=dma((2, half)), gf_recv=dma((2, half)),
         zr_send=dma((seq,)), zr_recv=dma((seq,)), za_send=dma((seq,)), za_recv=dma((seq,)),
     )
     whole = pl.BlockSpec(memory_space=pltpu.VMEM)

time: 66.3 us -> 57.9 us (0.87)
  Pallas kernels: 65.5 us -> 57 us
    pallas_call x1, Pallas kernels: 63.2 us -> 54.7 us  [body(): pl.pallas_call(functools.partial(kernel, dp, seq, heads, scale), out_shap...]
where the time goes in v5:
time: 57.9 us; the launch traced here: 57.7 us
  Pallas kernels  57 us (98%)
  between operations  0.64 us (1%)
    pallas_call x1, Pallas kernels, body(): pl.pallas_call(functools.partial(kernel, dp, seq, heads, scale), out_shap...  54.7 us
    pallas_call x1, Pallas kernels, body(): pl.pallas_call(place, out_shape=tuple((jax.ShapeDtypeStruct(part.shape, p...  2.31 us

profile of v5, /device:TPU:0, one launch (start us, length us, event | category | flops | bytes accessed | tf_op | source)
XLA Modules:
  0.0 57.7 jit_solution(14616763158620663909)
XLA Ops:
  0.6 54.7 %mixer_backward.1 = (bf16[128,2560]{1,0:T(8,128)(2,1)}, bf16[128,2560]{1,0:T(8,128)(2,1)}, f32[320,128]{1,0:T(8,128)}, f32[40,320]{1,0:T(8,128)}) custom-call(bf16[128,2560]{1,0:T(8,128)(2,1)} %bitcast.10, bf16[128,2560]{1,0:T(8,128)(2,1)} %bitcast.11, bf16[128,2560]{1,0:T(8,128)(2,1)} %bitcast.12, bf16[320,128]{1,0:T(8,128)(2,1)} %wbc_ref.1, ...), custom_call_target="tpu_custom_call" | custom-call | tf_op jit(solution)/shard_map/mixer_backward/pallas_call | solution.py:599
  55.4 2.3 %place_results.1 = (bf16[128,2560]{1,0:T(8,128)(2,1)}, bf16[128,2560]{1,0:T(8,128)(2,1)}, f32[320,128]{1,0:T(8,128)}, f32[40,320]{1,0:T(8,128)}) custom-call(bf16[128,2560]{1,0:T(8,128)(2,1)} %get-tuple-element.12.refs_0_, bf16[128,2560]{1,0:T(8,128)(2,1)} %get-tuple-element.13.refs_1_, f32[320,128]{1,0:T(8,128)} %get-tuple-element.14.refs_2_, ...), custom_call_target="tpu_custom_call" | custom-call | tf_op jit(solution)/shard_map/place_results/pallas_call | solution.py:619

commit v6 on v5

--- a/solution.py
+++ b/solution.py
@@ -226,6 +226,8 @@
         return result
 
     def lanes(c):
+        if isinstance(c, int):
+            return slice(c * CHUNK, (c + 1) * CHUNK)
         return pl.ds(pl.multiple_of(c * CHUNK, CHUNK), CHUNK)
 
     def chain_copy(way, c):
@@ -281,20 +283,20 @@
         return jnp.where(low_half, tile, turned), jnp.where(low_half, turned, tile)
 
     def tile_work(tile):
-        ts = pl.ds(pl.multiple_of(tile * LANES, LANES), LANES)
+        ts = slice(tile * LANES, (tile + 1) * LANES)
         g_tile = g_ref[:, ts].astype(F32)
         inter = inter_s[...]
         cums, steps = by_head(cum_w[:, ts]), by_head(step_w[:, ts])
         mixes, grads, sums = [], [], []
         for part in range(per_tile):
             head = tile * per_tile + part
-            gap = cumt_s[pl.ds(head, 1), :] - cums[part]
+            gap = cumt_s[head : head + 1, :] - cums[part]
             weights = jnp.exp(jnp.where(later, gap, -1e30))
             mine = low_half if part == 0 else jnp.logical_not(low_half)
             g_part = jnp.where(mine, g_tile, 0.0).astype(BF16)
             shared = m_s[head] * steps[part] * weights
             sums.append(shared)
-            rows_s[pl.ds(head, 1), :] = jnp.sum(shared * inter, axis=0, keepdims=True)
+            rows_s[head : head + 1, :] = jnp.sum(shared * inter, axis=0, keepdims=True)
             mixes += list(halves(inter * weights))
             grads += [g_part, g_part]
         ig_acc[...] += sum(sums[1:], sums[0])
@@ -341,24 +343,25 @@
     red_s[...] = jnp.zeros_like(red_s)
     tiles = CHUNK // LANES
 
-    local_work(0)
-    chain_start(0)
-
-    @pl.loop(0, chunks + max(last - 1, 0))
-    def _(s):
-        forward, back = s - (z - 1), s - (last - 1 - z)
-
-        @pl.when(s < chunks)
-        def _():
-            local_work(jnp.minimum(s + 1, chunks - 1))
-            for tile in range(tiles):
-                tile_work(s * tiles + tile)
-
-        @pl.when(s < chunks - 1)
-        def _():
-            chain_start(s + 1)
-
-        if seq > 1:
+    for c in range(chunks):
+        local_work(c)
+        chain_start(c)
+
+    steps = chunks + last
+    budget = -(-(chunks * tiles + 2 * chunks) // steps)
+    done = 0
+    for s in range(steps):
+        due = budget if s < last else max(budget - 2, 0)
+        if s == steps - 1:
+            due = chunks * tiles
+        for tile in range(done, min(done + due, chunks * tiles)):
+            tile_work(tile)
+        done = min(done + due, chunks * tiles)
+        if s >= last:
+            carried_work(s - last)
+        if seq > 1 and s < steps - 1:
+            forward, back = s - (z - 1), s - (last - 1 - z)
+
             @pl.when(jnp.logical_and(z > 0, jnp.logical_and(forward >= 0, forward < chunks)))
             def _():
                 chain_hop(0, forward)
@@ -366,12 +369,6 @@
             @pl.when(jnp.logical_and(z < last, jnp.logical_and(back >= 0, back < chunks)))
             def _():
                 chain_hop(1, back)
-
-        both = s - jnp.maximum(z, last - z) + min(last, 1)
-
-        @pl.when(jnp.logical_and(both >= 0, both < chunks))
-        def _():
-            carried_work(both)
 
     store_hg = pltpu.make_async_copy(hg_ref, hg_hbm, out_sem.at[0])
     store_hg.start()

time: 57.9 us -> 56.2 us (0.971)
  Pallas kernels: 57 us -> 55.4 us
    pallas_call x1, Pallas kernels: 54.7 us -> 53.1 us  [body(): pl.pallas_call(functools.partial(kernel, dp, seq, heads, scale), out_shap...]
where the time goes in v6:
time: 56.2 us; the launch traced here: 56 us
  Pallas kernels  55.4 us (99%)
  between operations  0.64 us (1%)
    pallas_call x1, Pallas kernels, body(): pl.pallas_call(functools.partial(kernel, dp, seq, heads, scale), out_shap...  53.1 us
    pallas_call x1, Pallas kernels, body(): pl.pallas_call(place, out_shape=tuple((jax.ShapeDtypeStruct(part.shape, p...  2.31 us

profile of v6, /device:TPU:0, one launch (start us, length us, event | category | flops | bytes accessed | tf_op | source)
XLA Modules:
  0.0 56.0 jit_solution(11869385760431162989)
XLA Ops:
  0.6 53.1 %mixer_backward.1 = (bf16[128,2560]{1,0:T(8,128)(2,1)}, bf16[128,2560]{1,0:T(8,128)(2,1)}, f32[320,128]{1,0:T(8,128)}, f32[40,320]{1,0:T(8,128)}) custom-call(bf16[128,2560]{1,0:T(8,128)(2,1)} %bitcast.10, bf16[128,2560]{1,0:T(8,128)(2,1)} %bitcast.11, bf16[128,2560]{1,0:T(8,128)(2,1)} %bitcast.12, bf16[320,128]{1,0:T(8,128)(2,1)} %wbc_ref.1, ...), custom_call_target="tpu_custom_call" | custom-call | tf_op jit(solution)/shard_map/mixer_backward/pallas_call | solution.py:596
  53.7 2.3 %place_results.1 = (bf16[128,2560]{1,0:T(8,128)(2,1)}, bf16[128,2560]{1,0:T(8,128)(2,1)}, f32[320,128]{1,0:T(8,128)}, f32[40,320]{1,0:T(8,128)}) custom-call(bf16[128,2560]{1,0:T(8,128)(2,1)} %get-tuple-element.12.refs_0_, bf16[128,2560]{1,0:T(8,128)(2,1)} %get-tuple-element.13.refs_1_, f32[320,128]{1,0:T(8,128)} %get-tuple-element.14.refs_2_, ...), custom_call_target="tpu_custom_call" | custom-call | tf_op jit(solution)/shard_map/place_results/pallas_call | solution.py:616

commit v7 on v6

--- a/solution.py
+++ b/solution.py
@@ -347,28 +347,30 @@
         local_work(c)
         chain_start(c)
 
-    steps = chunks + last
+    lag = max(last - 1, 0)
+    steps = chunks + lag
     budget = -(-(chunks * tiles + 2 * chunks) // steps)
     done = 0
     for s in range(steps):
-        due = budget if s < last else max(budget - 2, 0)
+        if seq > 1:
+            forward, back = s - (z - 1), s - (last - 1 - z)
+
+            @pl.when(jnp.logical_and(z > 0, jnp.logical_and(forward >= 0, forward < chunks)))
+            def _():
+                chain_hop(0, forward)
+
+            @pl.when(jnp.logical_and(z < last, jnp.logical_and(back >= 0, back < chunks)))
+            def _():
+                chain_hop(1, back)
+
+        due = budget if s < lag else max(budget - 2, 0)
         if s == steps - 1:
             due = chunks * tiles
         for tile in range(done, min(done + due, chunks * tiles)):
             tile_work(tile)
         done = min(done + due, chunks * tiles)
-        if s >= last:
-            carried_work(s - last)
-        if seq > 1 and s < steps - 1:
-            forward, back = s - (z - 1), s - (last - 1 - z)
-
-            @pl.when(jnp.logical_and(z > 0, jnp.logical_and(forward >= 0, forward < chunks)))
-            def _():
-                chain_hop(0, forward)
-
-            @pl.when(jnp.logical_and(z < last, jnp.logical_and(back >= 0, back < chunks)))
-            def _():
-                chain_hop(1, back)
+        if s >= lag:
+            carried_work(s - lag)
 
     store_hg = pltpu.make_async_copy(hg_ref, hg_hbm, out_sem.at[0])
     store_hg.start()

time: 56.2 us -> 56.3 us (level)
  no operation moved by 1% of the time
where the time goes in v7:
time: 56.3 us; the launch traced here: 56.1 us
  Pallas kernels  55.5 us (99%)
  between operations  0.64 us (1%)
    pallas_call x1, Pallas kernels, body(): pl.pallas_call(functools.partial(kernel, dp, seq, heads, scale), out_shap...  53.2 us
    pallas_call x1, Pallas kernels, body(): pl.pallas_call(place, out_shape=tuple((jax.ShapeDtypeStruct(part.shape, p...  2.31 us

profile of v7, /device:TPU:0, one launch (start us, length us, event | category | flops | bytes accessed | tf_op | source)
XLA Modules:
  0.0 56.1 jit_solution(588302701851719736)
XLA Ops:
  0.6 53.2 %mixer_backward.1 = (bf16[128,2560]{1,0:T(8,128)(2,1)}, bf16[128,2560]{1,0:T(8,128)(2,1)}, f32[320,128]{1,0:T(8,128)}, f32[40,320]{1,0:T(8,128)}) custom-call(bf16[128,2560]{1,0:T(8,128)(2,1)} %bitcast.10, bf16[128,2560]{1,0:T(8,128)(2,1)} %bitcast.11, bf16[128,2560]{1,0:T(8,128)(2,1)} %bitcast.12, bf16[320,128]{1,0:T(8,128)(2,1)} %wbc_ref.1, ...), custom_call_target="tpu_custom_call" | custom-call | tf_op jit(solution)/shard_map/mixer_backward/pallas_call | solution.py:598
  53.8 2.3 %place_results.1 = (bf16[128,2560]{1,0:T(8,128)(2,1)}, bf16[128,2560]{1,0:T(8,128)(2,1)}, f32[320,128]{1,0:T(8,128)}, f32[40,320]{1,0:T(8,128)}) custom-call(bf16[128,2560]{1,0:T(8,128)(2,1)} %get-tuple-element.12.refs_0_, bf16[128,2560]{1,0:T(8,128)(2,1)} %get-tuple-element.13.refs_1_, f32[320,128]{1,0:T(8,128)} %get-tuple-element.14.refs_2_, ...), custom_call_target="tpu_custom_call" | custom-call | tf_op jit(solution)/shard_map/place_results/pallas_call | solution.py:618

commit v8 on v7

--- a/solution.py
+++ b/solution.py
@@ -294,11 +294,14 @@
             weights = jnp.exp(jnp.where(later, gap, -1e30))
             mine = low_half if part == 0 else jnp.logical_not(low_half)
             g_part = jnp.where(mine, g_tile, 0.0).astype(BF16)
-            shared = m_s[head] * steps[part] * weights
-            sums.append(shared)
-            rows_s[head : head + 1, :] = jnp.sum(shared * inter, axis=0, keepdims=True)
-            mixes += list(halves(inter * weights))
-            grads += [g_part, g_part]
+            scaled = m_s[head] * steps[part]
+            sums.append(scaled * weights)
+            mixing = (inter * weights).astype(BF16)
+            rows_s[head : head + 1, :] = jnp.sum(
+                scaled * mixing.astype(F32), axis=0, keepdims=True
+            )
+            mixes.append(mixing)
+            grads.append(g_part)
         ig_acc[...] += sum(sums[1:], sums[0])
         sgrad[:, ts] = mm(jnp.concatenate(mixes, axis=1), jnp.concatenate(grads, axis=0))
 

time: 56.3 us -> 56.1 us (level)
  no operation moved by 1% of the time
where the time goes in v8:
time: 56.1 us; the launch traced here: 55.9 us
  Pallas kernels  55.3 us (99%)
  between operations  0.64 us (1%)
    pallas_call x1, Pallas kernels, body(): pl.pallas_call(functools.partial(kernel, dp, seq, heads, scale), out_shap...  53 us
    pallas_call x1, Pallas kernels, body(): pl.pallas_call(place, out_shape=tuple((jax.ShapeDtypeStruct(part.shape, p...  2.31 us

profile of v8, /device:TPU:0, one launch (start us, length us, event | category | flops | bytes accessed | tf_op | source)
XLA Modules:
  0.0 55.9 jit_solution(10061262630714005581)
XLA Ops:
  0.6 53.0 %mixer_backward.1 = (bf16[128,2560]{1,0:T(8,128)(2,1)}, bf16[128,2560]{1,0:T(8,128)(2,1)}, f32[320,128]{1,0:T(8,128)}, f32[40,320]{1,0:T(8,128)}) custom-call(bf16[128,2560]{1,0:T(8,128)(2,1)} %bitcast.10, bf16[128,2560]{1,0:T(8,128)(2,1)} %bitcast.11, bf16[128,2560]{1,0:T(8,128)(2,1)} %bitcast.12, bf16[320,128]{1,0:T(8,128)(2,1)} %wbc_ref.1, ...), custom_call_target="tpu_custom_call" | custom-call | tf_op jit(solution)/shard_map/mixer_backward/pallas_call | solution.py:601
  53.6 2.3 %place_results.1 = (bf16[128,2560]{1,0:T(8,128)(2,1)}, bf16[128,2560]{1,0:T(8,128)(2,1)}, f32[320,128]{1,0:T(8,128)}, f32[40,320]{1,0:T(8,128)}) custom-call(bf16[128,2560]{1,0:T(8,128)(2,1)} %get-tuple-element.12.refs_0_, bf16[128,2560]{1,0:T(8,128)(2,1)} %get-tuple-element.13.refs_1_, f32[320,128]{1,0:T(8,128)} %get-tuple-element.14.refs_2_, ...), custom_call_target="tpu_custom_call" | custom-call | tf_op jit(solution)/shard_map/place_results/pallas_call | solution.py:621
